TPU v7x, 32 devices: a whole 2x2x4 slice. The times are simulated.
32 devices in a mesh: gy: 8 (over y, x, core), gz: 4 (over z).
Axes of the slice: x: 2, y: 2, z: 4, core: 2. Of those that a mesh axis runs over, the one named last changes fastest.
Arguments:
- coarse: float32 [8, 1, 256, 256], P(None, None, 'gy', 'gz'), may hold values from 0 to 1
- labels: int32 [2, 512, 512], P(None, 'gy', 'gz'), may hold values from 0 to 7
- mobility: float32 [8], replicated, may hold values from 0.5 to 2
Outputs:
- phase_field: float32 [8, 2, 512, 512], P(None, None, 'gy', 'gz')
All inputs are finite; a program needn't handle non-finite values.
Results may differ from a plain program's by a relative error of at most 0.0001.
Values sent between devices are 32-bit elements; how exact they have to be, the bound alone decides.
A program may use at most 64 MiB of HBM per device.

v0:
```python
import jax
import jax.numpy as jnp
from jax import lax
from jax.sharding import PartitionSpec as P

ITERS = 2


STEP = 0.075
GAMMA = 0.5
PIN = 1.0


def padded_2(cells, sides, width):
    for axis, dim in sides:
        count = lax.axis_size(axis)
        head = lax.slice_in_dim(cells, 0, width, axis=dim)
        tail = lax.slice_in_dim(cells, cells.shape[dim] - width, cells.shape[dim], axis=dim)
        cells = jnp.concatenate(
            [
                lax.ppermute(tail, axis, [(i, (i + 1) % count) for i in range(count)]),
                cells,
                lax.ppermute(head, axis, [((i + 1) % count, i) for i in range(count)]),
            ],
            axis=dim,
        )
    return cells


def refine(field, axis):
    count = field.shape[axis]
    lower = lax.slice_in_dim(field, 0, count - 1, axis=axis)
    upper = lax.slice_in_dim(field, 1, count, axis=axis)
    odd_cells = 0.75 * lower + 0.25 * upper
    even_cells = 0.75 * upper + 0.25 * lower
    paired = jnp.stack([odd_cells, even_cells], axis=axis + 1)
    shape = list(field.shape)
    shape[axis] = 2 * (count - 1)
    return paired.reshape(shape)


def advance(padded, labels, mobility):
    center = padded[:, :, 1:-1, 1:-1]
    lap = jnp.roll(center, 1, 1) + jnp.roll(center, -1, 1)
    lap = lap + padded[:, :, 2:, 1:-1] + padded[:, :, :-2, 1:-1]
    lap = lap + padded[:, :, 1:-1, 2:] + padded[:, :, 1:-1, :-2] - 6.0 * center
    phases = jnp.arange(center.shape[0], dtype=jnp.int32)
    onehot = (labels[None] == phases[:, None, None, None]).astype(jnp.float32)
    squared = center * center
    squares = jnp.sum(squared, axis=0, keepdims=True)
    drive = (
        center * (1.0 - squared)
        - 2.0 * GAMMA * center * (squares - squared)
        + PIN * (onehot - center)
    )
    return center + STEP * mobility[:, None, None, None] * (lap + drive)


def fine_faces(phase):
    return padded_2(phase, (("gy", 2), ("gz", 3)), 1)


def shards(coarse, labels, mobility):
    width = 1
    padded = padded_2(coarse, (("gy", 2), ("gz", 3)), width)
    padded = jnp.pad(padded, ((0, 0), (1, 1), (0, 0), (0, 0)), mode="wrap")
    fine = refine(refine(refine(padded, 1), 2), 3)[:, 1:-1]
    rim = 2 * width - 1
    phase = fine[:, :, rim:-rim, rim:-rim]
    for step in range(ITERS):
        phase = advance(fine_faces(phase), labels, mobility)
    return phase


def solution(mesh):
    in_specs = (P(None, None, "gy", "gz"), P(None, "gy", "gz"), P())
    out_specs = P(None, None, "gy", "gz")
    return jax.shard_map(shards, mesh=mesh, in_specs=in_specs, out_specs=out_specs, check_vma=False)
```

profile of v0, /device:TPU:0, one launch (start us, length us, event | category | flops | bytes accessed | tf_op | source)
XLA Modules:
  0.0 72.7 jit_solution(13343388254340923318)
XLA Ops:
  0.0 0.8 %fusion.34 = (f32[8,1,1,64]{3,2,1,0:T(1,128)S(1)}, f32[8,1,1,64]{3,2,1,0:T(1,128)S(1)}) fusion(f32[8,1,32,64]{3,2,1,0:T(8,128)} %param.3), kind=kLoop, calls=%fused_computation.73 | loop fusion | bytes 8192 | tf_op jit(solution)/shard_map/slice | solution.py:18
  0.8 0.5 collective-permute-start
  1.2 2.9 %collective-permute-start.1 = (f32[8,1,1,64]{3,2,1,0:T(1,128)S(1)}, f32[8,1,1,64]{3,2,1,0:T(1,128)S(1)}, u32[]{:S(2)}, u32[]{:S(2)}) collective-permute-start(f32[8,1,1,64]{3,2,1,0:T(1,128)S(1)} %get-tuple-element.24), channel_id=1, source_target_pairs={{4,0},{8,4},{12,8},{16,12},{20,16},{24,20},{28,24},{0,28},{5,1},{9... | collective-permute-start | bytes 6152 | tf_op jit(solution)/shard_map/ppermute | solution.py:23
  4.2 1.2 %collective-permute-done = f32[8,1,1,64]{3,2,1,0:T(1,128)S(1)} collective-permute-done((f32[8,1,1,64]{3,2,1,0:T(1,128)S(1)}, f32[8,1,1,64]{3,2,1,0:T(1,128)S(1)}, u32[]{:S(2)}, u32[]{:S(2)}) %collective-permute-start) | collective-permute-done | bytes 2080 | tf_op jit(solution)/shard_map/ppermute | solution.py:21
  5.5 0.9 %pad_maximum_fusion.19 = f32[8,1,34,64]{3,2,1,0:T(8,128)S(1)} fusion(f32[8,1,1,64]{3,2,1,0:T(1,128)S(1)} %collective-permute-done.1, f32[8,1,32,64]{3,2,1,0:T(8,128)} %param.3, f32[8,1,1,64]{3,2,1,0:T(1,128)S(1)} %collective-permute-done), kind=kLoop, calls=%fused_computation.58 | loop fusion | flops 34816 | bytes 139264 | tf_op jit(solution)/shard_map/concatenate | solution.py:19
  6.5 2.3 %collective-permute-start.2 = (f32[8,1,34,1]{3,2,1,0:T(8,128)S(1)}, f32[8,1,34,1]{3,2,1,0:T(8,128)S(1)}, u32[]{:S(2)}, u32[]{:S(2)}) collective-permute-start(f32[8,1,34,1]{3,2,1,0:T(8,128)S(1)} %get-tuple-element.21), channel_id=1, source_target_pairs={{0,1},{1,2},{2,3},{3,0},{4,5},{5,6},{6,7},{7,4},{8,9},{9,10},{10,1... | collective-permute-start | bytes 3272 | tf_op jit(solution)/shard_map/ppermute | solution.py:21
  8.9 2.1 %collective-permute-start.3 = (f32[8,1,34,1]{3,2,1,0:T(8,128)S(1)}, f32[8,1,34,1]{3,2,1,0:T(8,128)S(1)}, u32[]{:S(2)}, u32[]{:S(2)}) collective-permute-start(f32[8,1,34,1]{3,2,1,0:T(8,128)S(1)} %get-tuple-element.22), channel_id=1, source_target_pairs={{1,0},{2,1},{3,2},{0,3},{5,4},{6,5},{7,6},{4,7},{9,8},{10,9},{11,1... | collective-permute-start | bytes 3272 | tf_op jit(solution)/shard_map/ppermute | solution.py:23
  11.0 5.1 %collective-permute-done.2 = f32[8,1,34,1]{3,2,1,0:T(8,128)S(1)} collective-permute-done((f32[8,1,34,1]{3,2,1,0:T(8,128)S(1)}, f32[8,1,34,1]{3,2,1,0:T(8,128)S(1)}, u32[]{:S(2)}, u32[]{:S(2)}) %collective-permute-start.2) | collective-permute-done | bytes 1120 | tf_op jit(solution)/shard_map/ppermute | solution.py:21
  16.1 2.8 %collective-permute-done.3 = f32[8,1,34,1]{3,2,1,0:T(8,128)S(1)} collective-permute-done((f32[8,1,34,1]{3,2,1,0:T(8,128)S(1)}, f32[8,1,34,1]{3,2,1,0:T(8,128)S(1)}, u32[]{:S(2)}, u32[]{:S(2)}) %collective-permute-start.3) | collective-permute-done | bytes 1120 | tf_op jit(solution)/shard_map/ppermute | solution.py:23
  18.9 1.1 %maximum_bitcast_fusion = f32[8,34,66]{2,1,0:T(8,128)S(1)} fusion(f32[8,1,34,1]{3,2,1,0:T(8,128)S(1)} %collective-permute-done.3, f32[8,1,1,64]{3,2,1,0:T(1,128)S(1)} %collective-permute-done.1, f32[8,1,32,64]{3,2,1,0:T(8,128)} %param.3, f32[8,1,1,64]{3,2,1,0:T(1,128)S(1)} %collective-permute-done, f32[8,1,34,1]{3,2,1,0:T(8,128)S(1)} %collective-permute-done.2), kind=kLoop, calls=%fused_computation.59 | loop fusion | flops 71808 | bytes 143616 | tf_op jit(solution)/shard_map/add | solution.py:34
  20.6 1.5 %pad_maximum_fusion = f32[8,4,66,65,2]{3,0,2,1,4:T(8,128)} fusion(f32[8,4,66,65,1]{3,0,2,1,4:T(8,128)S(1)} %get-tuple-element.14, f32[8,4,66,65,1]{3,0,2,1,4:T(8,128)S(1)} %get-tuple-element.13), kind=kLoop, calls=%fused_computation.2 | loop fusion | flops 274560 | bytes 2196480 | tf_op jit(solution)/shard_map/stack | solution.py:36
  22.1 2.5 %copy.15 = f32[8,4,66,65,2]{2,0,4,3,1:T(8,128)S(1)} copy(f32[8,4,66,65,2]{3,0,2,1,4:T(8,128)} %pad_maximum_fusion) | data formatting | bytes 2196480 | tf_op jit(solution)/shard_map/stack | solution.py:36
  24.6 1.6 %fusion.30 = (f32[8,2,1,128]{2,0,3,1:T(8,128)}, f32[8,2,1,128]{2,0,3,1:T(8,128)S(1)}) fusion(f32[8,4,66,130]{2,0,3,1:T(8,128)S(1)} %bitcast.13), kind=kLoop, calls=%fused_computation.69 | loop fusion | bytes 32768 | tf_op jit(solution)/shard_map/slice | solution.py:18
  26.2 1.6 %copy.18 = f32[8,2,1,128]{3,0,2,1:T(8,128)S(1)} copy(f32[8,2,1,128]{2,0,3,1:T(8,128)} %get-tuple-element.11) | data formatting | bytes 16384 | tf_op jit(solution)/shard_map/slice | solution.py:18
  28.1 1.7 %collective-permute-start.4 = (f32[8,2,1,128]{3,0,2,1:T(8,128)S(1)}, f32[8,2,1,128]{3,0,2,1:T(8,128)S(1)}, u32[]{:S(2)}, u32[]{:S(2)}) collective-permute-start(f32[8,2,1,128]{3,0,2,1:T(8,128)S(1)} %copy.16), channel_id=1, source_target_pairs={{4,0},{8,4},{12,8},{16,12},{20,16},{24,20},{28,24},{0,28},{5,1},{9... | collective-permute-start | bytes 24584 | tf_op jit(solution)/shard_map/ppermute | solution.py:23
  30.3 3.5 %collective-permute-done.5 = f32[8,2,1,128]{3,0,2,1:T(8,128)S(1)} collective-permute-done((f32[8,2,1,128]{3,0,2,1:T(8,128)S(1)}, f32[8,2,1,128]{3,0,2,1:T(8,128)S(1)}, u32[]{:S(2)}, u32[]{:S(2)}) %collective-permute-start.5) | collective-permute-done | bytes 8224 | tf_op jit(solution)/shard_map/ppermute | solution.py:21
  33.8 1.3 %copy.19 = f32[8,2,1,128]{2,0,3,1:T(8,128)} copy(f32[8,2,1,128]{3,0,2,1:T(8,128)S(1)} %collective-permute-done.5) | data formatting | bytes 16384 | tf_op jit(solution)/shard_map/ppermute | solution.py:21
  35.1 1.4 %copy.17 = f32[8,2,1,128]{2,0,3,1:T(8,128)} copy(f32[8,2,1,128]{3,0,2,1:T(8,128)S(1)} %collective-permute-done.4) | data formatting | bytes 16384 | tf_op jit(solution)/shard_map/ppermute | solution.py:23
  36.5 0.9 %pad_maximum_fusion.25 = (f32[8,2,66,1]{2,0,3,1:T(8,128)S(1)}, f32[8,2,66,1]{2,0,3,1:T(8,128)S(1)}) fusion(f32[8,2,1,128]{2,0,3,1:T(8,128)} %copy.17, f32[8,2,64,128]{2,0,3,1:T(8,128)S(1)} %slice.149, f32[8,2,1,128]{2,0,3,1:T(8,128)} %copy.19), kind=kLoop, calls=%fused_computation.65 | loop fusion | flops 4224 | bytes 549120 | tf_op jit(solution)/shard_map/slice | solution.py:17
  37.4 2.0 %collective-permute-start.6 = (f32[8,2,66,1]{2,0,3,1:T(8,128)S(1)}, f32[8,2,66,1]{2,0,3,1:T(8,128)S(1)}, u32[]{:S(2)}, u32[]{:S(2)}) collective-permute-start(f32[8,2,66,1]{2,0,3,1:T(8,128)S(1)} %get-tuple-element.7), channel_id=1, source_target_pairs={{1,0},{2,1},{3,2},{0,3},{5,4},{6,5},{7,6},{4,7},{9,8},{10,9},{11,1... | collective-permute-start | bytes 12680 | tf_op jit(solution)/shard_map/ppermute | solution.py:23
  39.9 1.3 %collective-permute-done.6 = f32[8,2,66,1]{2,0,3,1:T(8,128)S(1)} collective-permute-done((f32[8,2,66,1]{2,0,3,1:T(8,128)S(1)}, f32[8,2,66,1]{2,0,3,1:T(8,128)S(1)}, u32[]{:S(2)}, u32[]{:S(2)}) %collective-permute-start.6) | collective-permute-done | bytes 4256 | tf_op jit(solution)/shard_map/ppermute | solution.py:23
  41.1 3.7 %collective-permute-done.7 = f32[8,2,66,1]{2,0,3,1:T(8,128)S(1)} collective-permute-done((f32[8,2,66,1]{2,0,3,1:T(8,128)S(1)}, f32[8,2,66,1]{2,0,3,1:T(8,128)S(1)}, u32[]{:S(2)}, u32[]{:S(2)}) %collective-permute-start.7) | collective-permute-done | bytes 4256 | tf_op jit(solution)/shard_map/ppermute | solution.py:21
  44.9 10.9 %fusion.22 = f32[8,2,64,128]{2,0,3,1:T(8,128)S(1)} fusion(f32[8,2,64,128]{2,0,3,1:T(8,128)S(1)} %copy-done.1, f32[8,2,66,1]{2,0,3,1:T(8,128)S(1)} %collective-permute-done.7, f32[8,2,1,128]{2,0,3,1:T(8,128)S(1)} %copy-done.3, f32[8,2,1,128]{2,0,3,1:T(8,128)S(1)} %copy-done.2, f32[8,2,66,1]{2,0,3,1:T(8,128)S(1)} %collective-permute-done.6, ...), kind=kOutput, calls=%fused_computation.37 | output fusion | flops 3948551 | bytes 6963712 | tf_op jit(solution)/shard_map/sub | solution.py:53
  56.9 2.7 %collective-permute-start.8 = (f32[8,2,1,128]{3,0,2,1:T(8,128)S(1)}, f32[8,2,1,128]{3,0,2,1:T(8,128)S(1)}, u32[]{:S(2)}, u32[]{:S(2)}) collective-permute-start(f32[8,2,1,128]{3,0,2,1:T(8,128)S(1)} %copy.23), channel_id=1, source_target_pairs={{4,0},{8,4},{12,8},{16,12},{20,16},{24,20},{28,24},{0,28},{5,1},{9... | collective-permute-start | bytes 24584 | tf_op jit(solution)/shard_map/ppermute | solution.py:23
  59.5 1.0 %collective-permute-done.9 = f32[8,2,1,128]{3,0,2,1:T(8,128)S(1)} collective-permute-done((f32[8,2,1,128]{3,0,2,1:T(8,128)S(1)}, f32[8,2,1,128]{3,0,2,1:T(8,128)S(1)}, u32[]{:S(2)}, u32[]{:S(2)}) %collective-permute-start.9) | collective-permute-done | bytes 8224 | tf_op jit(solution)/shard_map/ppermute | solution.py:21
  60.5 0.4 copy.26
  60.9 0.4 copy.24
  61.4 2.0 %collective-permute-start.11 = (f32[8,2,66,1]{2,0,3,1:T(8,128)S(1)}, f32[8,2,66,1]{2,0,3,1:T(8,128)S(1)}, u32[]{:S(2)}, u32[]{:S(2)}) collective-permute-start(f32[8,2,66,1]{2,0,3,1:T(8,128)S(1)} %get-tuple-element.6), channel_id=1, source_target_pairs={{0,1},{1,2},{2,3},{3,0},{4,5},{5,6},{6,7},{7,4},{8,9},{9,10},{10,1... | collective-permute-start | bytes 12680 | tf_op jit(solution)/shard_map/ppermute | solution.py:21
  63.5 1.6 %collective-permute-done.10 = f32[8,2,66,1]{2,0,3,1:T(8,128)S(1)} collective-permute-done((f32[8,2,66,1]{2,0,3,1:T(8,128)S(1)}, f32[8,2,66,1]{2,0,3,1:T(8,128)S(1)}, u32[]{:S(2)}, u32[]{:S(2)}) %collective-permute-start.10) | collective-permute-done | bytes 4256 | tf_op jit(solution)/shard_map/ppermute | solution.py:23
  65.1 1.9 %collective-permute-done.11 = f32[8,2,66,1]{2,0,3,1:T(8,128)S(1)} collective-permute-done((f32[8,2,66,1]{2,0,3,1:T(8,128)S(1)}, f32[8,2,66,1]{2,0,3,1:T(8,128)S(1)}, u32[]{:S(2)}, u32[]{:S(2)}) %collective-permute-start.11) | collective-permute-done | bytes 4256 | tf_op jit(solution)/shard_map/ppermute | solution.py:21
  66.9 3.4 %fusion.14 = f32[8,2,64,128]{2,0,3,1:T(8,128)} fusion(f32[8,2,64,128]{2,0,3,1:T(8,128)S(1)} %fusion.22, f32[8,2,66,1]{2,0,3,1:T(8,128)S(1)} %collective-permute-done.11, f32[8,2,1,128]{2,0,3,1:T(8,128)S(1)} %copy.24, f32[8,2,1,128]{2,0,3,1:T(8,128)S(1)} %copy.26, f32[8,2,66,1]{2,0,3,1:T(8,128)S(1)} %collective-permute-done.10, ...), kind=kOutput, calls=%fused_computation.21 | output fusion | flops 3948551 | bytes 1663264 | tf_op jit(solution)/shard_map/sub | solution.py:53
  70.4 2.3 %copy.29 = f32[8,2,64,128]{3,2,1,0:T(8,128)} copy(f32[8,2,64,128]{2,0,3,1:T(8,128)} %fusion.14) | data formatting | bytes 1048576 | tf_op jit(solution)/shard_map/add | solution.py:56
  (36 shorter events, 3.3 us)
Async XLA Ops:
  0.8 4.6 %collective-permute-start = (f32[8,1,1,64]{3,2,1,0:T(1,128)S(1)}, f32[8,1,1,64]{3,2,1,0:T(1,128)S(1)}, u32[]{:S(2)}, u32[]{:S(2)}) collective-permute-start(f32[8,1,1,64]{3,2,1,0:T(1,128)S(1)} %get-tuple-element.23), channel_id=1, source_target_pairs={{0,4},{4,8},{8,12},{12,16},{16,20},{20,24},{24,28},{28,0},{1,5},{5... | collective-permute-start | bytes 6152 | tf_op jit(solution)/shard_map/ppermute | solution.py:21
  1.2 4.3 %collective-permute-start.1 = (f32[8,1,1,64]{3,2,1,0:T(1,128)S(1)}, f32[8,1,1,64]{3,2,1,0:T(1,128)S(1)}, u32[]{:S(2)}, u32[]{:S(2)}) collective-permute-start(f32[8,1,1,64]{3,2,1,0:T(1,128)S(1)} %get-tuple-element.24), channel_id=1, source_target_pairs={{4,0},{8,4},{12,8},{16,12},{20,16},{24,20},{28,24},{0,28},{5,1},{9... | collective-permute-start | bytes 6152 | tf_op jit(solution)/shard_map/ppermute | solution.py:23
  6.5 9.5 %collective-permute-start.2 = (f32[8,1,34,1]{3,2,1,0:T(8,128)S(1)}, f32[8,1,34,1]{3,2,1,0:T(8,128)S(1)}, u32[]{:S(2)}, u32[]{:S(2)}) collective-permute-start(f32[8,1,34,1]{3,2,1,0:T(8,128)S(1)} %get-tuple-element.21), channel_id=1, source_target_pairs={{0,1},{1,2},{2,3},{3,0},{4,5},{5,6},{6,7},{7,4},{8,9},{9,10},{10,1... | collective-permute-start | bytes 3272 | tf_op jit(solution)/shard_map/ppermute | solution.py:21
  8.9 10.0 %collective-permute-start.3 = (f32[8,1,34,1]{3,2,1,0:T(8,128)S(1)}, f32[8,1,34,1]{3,2,1,0:T(8,128)S(1)}, u32[]{:S(2)}, u32[]{:S(2)}) collective-permute-start(f32[8,1,34,1]{3,2,1,0:T(8,128)S(1)} %get-tuple-element.22), channel_id=1, source_target_pairs={{1,0},{2,1},{3,2},{0,3},{5,4},{6,5},{7,6},{4,7},{9,8},{10,9},{11,1... | collective-permute-start | bytes 3272 | tf_op jit(solution)/shard_map/ppermute | solution.py:23
  26.2 3.6 %copy-start.5 = (f32[8]{0:T(128)S(1)}, f32[8]{0:T(128)}, u32[]{:S(2)}) copy-start(f32[8]{0:T(128)} %param.5) | copy-start | bytes 100
  26.2 3.6 %copy-start.4 = (s32[2,64,128]{2,1,0:T(8,128)S(1)}, s32[2,64,128]{2,1,0:T(8,128)}, u32[]{:S(2)}) copy-start(s32[2,64,128]{2,1,0:T(8,128)} %param.4) | copy-start | bytes 196612
  28.1 7.0 %collective-permute-start.4 = (f32[8,2,1,128]{3,0,2,1:T(8,128)S(1)}, f32[8,2,1,128]{3,0,2,1:T(8,128)S(1)}, u32[]{:S(2)}, u32[]{:S(2)}) collective-permute-start(f32[8,2,1,128]{3,0,2,1:T(8,128)S(1)} %copy.16), channel_id=1, source_target_pairs={{4,0},{8,4},{12,8},{16,12},{20,16},{24,20},{28,24},{0,28},{5,1},{9... | collective-permute-start | bytes 24584 | tf_op jit(solution)/shard_map/ppermute | solution.py:23
  29.8 4.0 %collective-permute-start.5 = (f32[8,2,1,128]{3,0,2,1:T(8,128)S(1)}, f32[8,2,1,128]{3,0,2,1:T(8,128)S(1)}, u32[]{:S(2)}, u32[]{:S(2)}) collective-permute-start(f32[8,2,1,128]{3,0,2,1:T(8,128)S(1)} %copy.18), channel_id=1, source_target_pairs={{0,4},{4,8},{8,12},{12,16},{16,20},{20,24},{24,28},{28,0},{1,5},{5... | collective-permute-start | bytes 24584 | tf_op jit(solution)/shard_map/ppermute | solution.py:21
  30.3 7.1 %copy-start = (f32[8,2,64,128]{2,0,3,1:T(8,128)}, f32[8,2,64,128]{2,0,3,1:T(8,128)S(1)}, u32[]{:S(2)}) copy-start(f32[8,2,64,128]{2,0,3,1:T(8,128)S(1)} %slice.149) | copy-start | bytes 1572868
  36.5 8.4 %copy-start.3 = (f32[8,2,1,128]{2,0,3,1:T(8,128)S(1)}, f32[8,2,1,128]{2,0,3,1:T(8,128)}, u32[]{:S(2)}) copy-start(f32[8,2,1,128]{2,0,3,1:T(8,128)} %copy.17) | copy-start | bytes 24580
  37.4 7.5 %copy-start.2 = (f32[8,2,1,128]{2,0,3,1:T(8,128)S(1)}, f32[8,2,1,128]{2,0,3,1:T(8,128)}, u32[]{:S(2)}) copy-start(f32[8,2,1,128]{2,0,3,1:T(8,128)} %copy.19) | copy-start | bytes 24580
  37.4 7.5 %copy-start.1 = (f32[8,2,64,128]{2,0,3,1:T(8,128)S(1)}, f32[8,2,64,128]{2,0,3,1:T(8,128)}, u32[]{:S(2)}) copy-start(f32[8,2,64,128]{2,0,3,1:T(8,128)} %copy-done) | copy-start | bytes 1572868
  37.4 3.7 %collective-permute-start.6 = (f32[8,2,66,1]{2,0,3,1:T(8,128)S(1)}, f32[8,2,66,1]{2,0,3,1:T(8,128)S(1)}, u32[]{:S(2)}, u32[]{:S(2)}) collective-permute-start(f32[8,2,66,1]{2,0,3,1:T(8,128)S(1)} %get-tuple-element.7), channel_id=1, source_target_pairs={{1,0},{2,1},{3,2},{0,3},{5,4},{6,5},{7,6},{4,7},{9,8},{10,9},{11,1... | collective-permute-start | bytes 12680 | tf_op jit(solution)/shard_map/ppermute | solution.py:23
  39.4 5.4 %collective-permute-start.7 = (f32[8,2,66,1]{2,0,3,1:T(8,128)S(1)}, f32[8,2,66,1]{2,0,3,1:T(8,128)S(1)}, u32[]{:S(2)}, u32[]{:S(2)}) collective-permute-start(f32[8,2,66,1]{2,0,3,1:T(8,128)S(1)} %get-tuple-element.8), channel_id=1, source_target_pairs={{0,1},{1,2},{2,3},{3,0},{4,5},{5,6},{6,7},{7,4},{8,9},{9,10},{10,1... | collective-permute-start | bytes 12680 | tf_op jit(solution)/shard_map/ppermute | solution.py:21
  56.5 4.0 %collective-permute-start.9 = (f32[8,2,1,128]{3,0,2,1:T(8,128)S(1)}, f32[8,2,1,128]{3,0,2,1:T(8,128)S(1)}, u32[]{:S(2)}, u32[]{:S(2)}) collective-permute-start(f32[8,2,1,128]{3,0,2,1:T(8,128)S(1)} %copy.25), channel_id=1, source_target_pairs={{0,4},{4,8},{8,12},{12,16},{16,20},{20,24},{24,28},{28,0},{1,5},{5... | collective-permute-start | bytes 24584 | tf_op jit(solution)/shard_map/ppermute | solution.py:21
  56.9 4.0 %collective-permute-start.8 = (f32[8,2,1,128]{3,0,2,1:T(8,128)S(1)}, f32[8,2,1,128]{3,0,2,1:T(8,128)S(1)}, u32[]{:S(2)}, u32[]{:S(2)}) collective-permute-start(f32[8,2,1,128]{3,0,2,1:T(8,128)S(1)} %copy.23), channel_id=1, source_target_pairs={{4,0},{8,4},{12,8},{16,12},{20,16},{24,20},{28,24},{0,28},{5,1},{9... | collective-permute-start | bytes 24584 | tf_op jit(solution)/shard_map/ppermute | solution.py:23
  61.4 3.7 %collective-permute-start.10 = (f32[8,2,66,1]{2,0,3,1:T(8,128)S(1)}, f32[8,2,66,1]{2,0,3,1:T(8,128)S(1)}, u32[]{:S(2)}, u32[]{:S(2)}) collective-permute-start(f32[8,2,66,1]{2,0,3,1:T(8,128)S(1)} %get-tuple-element.5), channel_id=1, source_target_pairs={{1,0},{2,1},{3,2},{0,3},{5,4},{6,5},{7,6},{4,7},{9,8},{10,9},{11,1... | collective-permute-start | bytes 12680 | tf_op jit(solution)/shard_map/ppermute | solution.py:23
  61.4 5.5 %collective-permute-start.11 = (f32[8,2,66,1]{2,0,3,1:T(8,128)S(1)}, f32[8,2,66,1]{2,0,3,1:T(8,128)S(1)}, u32[]{:S(2)}, u32[]{:S(2)}) collective-permute-start(f32[8,2,66,1]{2,0,3,1:T(8,128)S(1)} %get-tuple-element.6), channel_id=1, source_target_pairs={{0,1},{1,2},{2,3},{3,0},{4,5},{5,6},{6,7},{7,4},{8,9},{9,10},{10,1... | collective-permute-start | bytes 12680 | tf_op jit(solution)/shard_map/ppermute | solution.py:21
where the time goes:
time: 73 us; the launch traced here: 72.7 us
  waiting for transfers between devices  22.1 us (30%)
  other arithmetic  19.4 us (27%)
  starting transfers between devices  16.3 us (22%)
  local copies, waits for them, and re-layouts  14.7 us (20%)
    ppermute x6, waiting for transfers between devices, padded_2(): lax.ppermute(tail, axis, [(i, (i + 1) % count) for i in range(count)])  16.4 us
    sub x2, other arithmetic, advance(): squares - squared  14.3 us
    ppermute x6, starting transfers between devices, padded_2(): lax.ppermute(head, axis, [((i + 1) % count, i) for i in range(count)])  11.4 us
    ppermute x6, waiting for transfers between devices, padded_2(): lax.ppermute(head, axis, [((i + 1) % count, i) for i in range(count)])  5.74 us
    ppermute x6, starting transfers between devices, padded_2(): lax.ppermute(tail, axis, [(i, (i + 1) % count) for i in range(count)])  4.92 us
    slice x6, local copies, waits for them, and re-layouts, padded_2(): lax.slice_in_dim(cells, cells.shape[dim] - width, cells.shape[dim], axis=...  4.75 us
    another operation x1, local copies, waits for them, and re-layouts, refine(): paired = jnp.stack([odd_cells, even_cells], axis=axis + 1)  2.51 us
    add x1, local copies, waits for them, and re-layouts, advance(): return center + STEP * mobility[:, None, None, None] * (lap + drive)  2.34 us
  transfers between devices with their start and end apart: 12, of which 10 were waited for; matrix products, arithmetic and copies ran while one was open for 4% of the time, Pallas kernels for 0%

commit v1 on v0

v1 whole, which is shorter than its diff:
```python
import functools

import jax
import jax.numpy as jnp
import numpy as np
from jax import lax
from jax.experimental import pallas as pl
from jax.experimental.pallas import tpu as pltpu
from jax.sharding import PartitionSpec as P

STEP = 0.075
MESH = pl.DeviceIdType.MESH
F32 = jnp.float32
BF16 = jnp.bfloat16


def taps(cell):
    i = cell // 2
    return ((i, 0.75), (i + 1 if cell % 2 else i - 1, 0.25))


def col_lane(col, nz):
    return col % (2 * nz)


def main_operator(nz):
    width = 2 * nz
    w = np.zeros((width, width), np.float32)
    for z in range(width):
        for c, a in taps(z):
            w[col_lane(c, nz), z] += a
    return w


def strip_operator(ny, nz):
    width = 2 * nz

    def where(r, c):
        if r == -1:
            return 2 * width + col_lane(c, nz)
        if r == ny:
            return 2 * width + (col_lane(c, nz) + 8) % width
        assert 0 <= r < ny
        if c in (0, 1):
            return 2 * r + c
        if c in (nz - 2, nz - 1):
            return 2 * ny + 2 * r + c - (nz - 2)
        if c in (nz, nz + 1):
            return width + 2 * r + c - nz
        assert c in (-2, -1)
        return width + 2 * ny + 2 * r + c + 2

    w = np.zeros((3 * width, 4 * width), np.float32)

    def put(y, z, out):
        for r, a in taps(y):
            for c, b in taps(z):
                w[where(r, c), out] += a * b

    for y in range(2 * ny):
        left, right = 2 * y, (2 * y - 1) % width
        for block, (zl, zr) in enumerate(((-2, width + 1), (-1, width), (0, width - 1))):
            put(y, zl, block * width + left)
            put(y, zr, block * width + right)
    put(-1, -1, 3 * width)
    put(-1, width, 3 * width + width - 1)
    put(2 * ny, -1, 3 * width + width - 2)
    put(2 * ny, width, 3 * width + width - 3)
    return w


def label_operator(ny, nz):
    width = 2 * nz
    w = np.zeros((2 * width, 2 * width), np.float32)
    for x in range(2):
        for y in range(2 * ny):
            w[x * 2 * ny + y, x * width + 2 * y] = 1
            w[width + x * 2 * ny + y, x * width + (2 * y - 1) % width] = 1
    return w


PARTS = (
    ((-1, 0), (0, 3), (0, 3)),
    ((1, 0), (3, 6), (3, 6)),
    ((0, -1), (6, 8), (6, 8)),
    ((0, 1), (8, 10), (8, 10)),
    ((-1, -1), (0, 2), (10, 12)),
    ((-1, 1), (0, 2), (12, 14)),
    ((1, -1), (3, 5), (14, 16)),
    ((1, 1), (3, 5), (16, 18)),
)
SLOTS = 19


def wide(x):
    return jnp.concatenate([x, jnp.zeros_like(x)], axis=-1)


def exchange(gy, gz, coarse_ref, labels_ref, out_ref, stage, send_sem, recv_sem):
    me_y, me_z = lax.axis_index("gy"), lax.axis_index("gz")

    def other(dy, dz):
        return (lax.rem(me_y + dy + gy, gy), lax.rem(me_z + dz + gz, gz))

    barrier = pltpu.get_barrier_semaphore()
    for (dy, dz), _, _ in PARTS:
        pl.semaphore_signal(barrier, inc=1, device_id=other(dy, dz), device_id_type=MESH)

    phases, _, ny, nz = coarse_ref.shape
    width = 2 * nz
    x = jnp.swapaxes(coarse_ref[:, 0], 0, 1)
    rows = [wide(x[r]) for r in range(ny)]
    lane = lax.broadcasted_iota(jnp.int32, (phases, width), 1)
    left = jnp.zeros((phases, width), F32)
    right = jnp.zeros((phases, width), F32)
    for r in range(ny):
        turned = rows[r] if r == 0 else pltpu.roll(rows[r], 2 * r, 1)
        left = jnp.where((lane >= 2 * r) & (lane < 2 * r + 2), turned, left)
        low = nz - 2 + 2 * r
        right = jnp.where((lane >= low) & (lane < low + 2), turned, right)
    right = pltpu.roll(right, (2 * ny - (nz - 2)) % width, 1)

    labels = labels_ref[...].astype(F32)
    flat = labels.reshape(-1, width)
    pick_lane = lax.broadcasted_iota(jnp.int32, (phases, width), 1)

    def column(z):
        pick = (pick_lane == z).astype(BF16)
        return lax.dot_general(
            pick, flat.astype(BF16), (((1,), (1,)), ((), ())), preferred_element_type=F32
        )

    stage[0] = rows[0]
    stage[1] = rows[1]
    stage[2, 0:2] = labels[:, 0]
    stage[3] = rows[ny - 2]
    stage[4] = rows[ny - 1]
    stage[5, 0:2] = labels[:, 2 * ny - 1]
    stage[6] = left
    stage[7] = column(0)
    stage[8] = right
    stage[9] = column(width - 1)
    out_ref[SLOTS - 1] = left + right

    pl.semaphore_wait(barrier, len(PARTS))
    copies = []
    for n, ((dy, dz), (s0, s1), (d0, d1)) in enumerate(PARTS):
        copy = pltpu.make_async_remote_copy(
            src_ref=stage.at[s0:s1],
            dst_ref=out_ref.at[d0:d1],
            send_sem=send_sem.at[n],
            recv_sem=recv_sem.at[n],
            device_id=other(dy, dz),
            device_id_type=MESH,
        )
        copy.start()
        copies.append(copy)
    for copy in copies:
        copy.wait()


def exact_dot(x, w):
    high = x.astype(BF16)
    low = (x - high.astype(F32)).astype(BF16)
    return jnp.dot(high, w, preferred_element_type=F32) + jnp.dot(low, w, preferred_element_type=F32)


def relax(coarse_ref, labels_ref, mobility_ref, got, main_ref, strip_ref, label_ref, out_ref, p1):
    phases, _, ny, nz = coarse_ref.shape
    width = 2 * nz
    fy = 2 * ny
    shape = (phases, width)
    lane = lax.broadcasted_iota(jnp.int32, shape, 1)
    phase_id = lax.broadcasted_iota(jnp.int32, shape, 0)
    phase_f = phase_id.astype(F32)
    rate = jnp.zeros(shape, F32)
    for p in range(phases):
        rate = jnp.where(phase_id == p, STEP * mobility_ref[p], rate)
    first, last = lane == 0, lane == width - 1
    ends = first | last

    def turn(v, by):
        return pltpu.roll(v, by % width, 1) if by % width else v

    def total(v):
        return jnp.broadcast_to(jnp.sum(v * v, axis=0, keepdims=True), shape)

    def around(c, side):
        return jnp.where(first, side, turn(c, 1)) + jnp.where(last, side, turn(c, -1))

    halo_right = (lane >= nz) & (lane < nz + 2)
    halo_left = lane >= width - 2

    def edge(row, from_left, from_right, left_by=nz, right_by=nz):
        v = jnp.where(halo_right, turn(from_right, right_by), row)
        return jnp.where(halo_left, turn(from_left, left_by), v)

    below = [edge(got[n], got[12 + n], got[10 + n]) for n in range(2)]
    above = [edge(got[3 + n], got[16 + n], got[14 + n]) for n in range(2)]
    x = jnp.swapaxes(coarse_ref[:, 0], 0, 1)
    x = jnp.concatenate([x, jnp.zeros_like(x)], axis=-1)
    top = edge(x[0], got[8], got[6], width - 2 - 2 * ny, nz)
    low = 2 * (ny - 1)
    bottom = edge(x[ny - 1], got[8], got[6], width - 2 - 2 * ny - low, nz - low)
    rows = jnp.concatenate(
        [jnp.stack([*above, top]), x[1 : ny - 1], jnp.stack([bottom, *below])], axis=0
    )
    fine_z = exact_dot(rows.reshape(-1, width), main_ref[...]).reshape(ny + 4, phases, width)

    beside = jnp.where(lane < 2 * ny, got[6], got[8])
    near = (lane < 4) | (lane >= nz - 4) & (lane < nz + 4) | (lane >= width - 4)
    rim = jnp.where(near, above[1], turn(below[0], 8))
    strips = exact_dot(jnp.concatenate([got[SLOTS - 1], beside, rim], axis=1), strip_ref[...])
    outer, side, inner, corner = (strips[:, n * width : (n + 1) * width] for n in range(4))
    near_labels = jnp.concatenate([got[9], got[7]], axis=1).astype(BF16)
    strip_labels = jnp.dot(near_labels, label_ref[...], preferred_element_type=F32)
    up = jnp.where(ends, corner, turn(side, 2))
    down = jnp.where((lane == width - 2) | (lane == width - 3), corner, turn(side, -2))
    side_base = side + rate * (outer + inner + up + down - side * (4.0 + total(side)))
    side1 = [
        side_base + jnp.where(strip_labels[:, n * width : (n + 1) * width] == phase_f, rate, 0.0)
        for n in range(2)
    ]

    def fine_row(y):
        (r0, a), (r1, b) = taps(y)
        v = a * fine_z[r0 + 2] + b * fine_z[r1 + 2]
        return jnp.where(ends, turn(inner, -2 * y), v) if 0 <= y < fy else v

    def label_row(n, y):
        if y < 0:
            row = got[5, n : n + 1]
        elif y >= fy:
            row = got[2, n : n + 1]
        else:
            return jnp.broadcast_to(labels_ref[n, y : y + 1], shape) == phase_id
        return jnp.broadcast_to(row, shape) == phase_f

    def pinned(n, y):
        return jnp.where(label_row(n, y), rate, 0.0)

    prev, cur = fine_row(-2), fine_row(-1)
    for y in range(-1, fy + 1):
        nxt = fine_row(y + 1)
        if y < 0:
            beside_row = corner
        elif y == fy:
            beside_row = turn(corner, 2)
        else:
            beside_row = turn(side, -2 * y)
        base = cur + rate * (prev + nxt + around(cur, beside_row) - cur * (4.0 + total(cur)))
        for n in range(2):
            p1[n, y + 1] = base + pinned(n, y)
        prev, cur = cur, nxt

    for block in range(fy // 8):
        done = [[], []]
        for y in range(8 * block, 8 * block + 8):
            both = [p1[n, y + 1] for n in range(2)]
            for n in range(2):
                c = both[n]
                near = p1[n, y] + p1[n, y + 2] + around(c, turn(side1[n], -2 * y))
                near = near + 2.0 * both[1 - n]
                done[n].append(c + rate * (near - c * (6.0 + total(c))) + pinned(n, y))
        for n in range(2):
            out_ref[:, n, 8 * block : 8 * block + 8] = jnp.swapaxes(jnp.stack(done[n]), 0, 1)


def shards(gy, gz, coarse, labels, mobility):
    phases, planes, ny, nz = coarse.shape
    assert planes == 1 and labels.shape == (2, 2 * ny, 2 * nz) and ny <= nz // 2 and phases == 8
    width = 2 * nz
    vmem = pl.BlockSpec(memory_space=pltpu.VMEM)
    got = pl.pallas_call(
        functools.partial(exchange, gy, gz),
        out_shape=jax.ShapeDtypeStruct((SLOTS, phases, width), F32),
        in_specs=[vmem] * 2,
        out_specs=vmem,
        scratch_shapes=[
            pltpu.VMEM((10, phases, width), F32),
            pltpu.SemaphoreType.DMA((len(PARTS),)),
            pltpu.SemaphoreType.DMA((len(PARTS),)),
        ],
        compiler_params=pltpu.CompilerParams(collective_id=0, has_side_effects=True),
        name="exchange",
    )(coarse, labels)
    weights = [
        jnp.asarray(w, BF16)
        for w in (main_operator(nz), strip_operator(ny, nz), label_operator(ny, nz))
    ]
    return pl.pallas_call(
        relax,
        out_shape=jax.ShapeDtypeStruct((phases, 2, 2 * ny, width), F32),
        in_specs=[vmem] * 2 + [pl.BlockSpec(memory_space=pltpu.SMEM)] + [vmem] * 4,
        out_specs=vmem,
        scratch_shapes=[pltpu.VMEM((2, 2 * ny + 2, phases, width), F32)],
        compiler_params=pltpu.CompilerParams(vmem_limit_bytes=16 * 2**20),
        name="relax",
    )(coarse, labels, mobility, got, *weights)


def solution(mesh):
    in_specs = (P(None, None, "gy", "gz"), P(None, "gy", "gz"), P())
    out_specs = P(None, None, "gy", "gz")
    fn = functools.partial(shards, mesh.shape["gy"], mesh.shape["gz"])
    return jax.shard_map(fn, mesh=mesh, in_specs=in_specs, out_specs=out_specs, check_vma=False)
```

time: 73 us -> 16.3 us (0.22)
  waiting for transfers between devices: 22.1 us -> 0 us
  other arithmetic: 19.4 us -> 0 us
  starting transfers between devices: 16.3 us -> 0 us
  Pallas kernels: 0 us -> 13.2 us
  local copies, waits for them, and re-layouts: 14.7 us -> 2.8 us
    ppermute x12 -> x0, waiting for transfers between devices: 22.1 us -> none  [the longest x6 16.4 us: padded_2(): lax.ppermute(tail, axis, [(i, (i + 1) % count) for i in range(count)])]
    ppermute x12 -> x0, starting transfers between devices: 16.3 us -> none  [the longest x6 11.4 us: padded_2(): lax.ppermute(head, axis, [((i + 1) % count, i) for i in range(count)])]
    sub x2 -> x0, other arithmetic: 14.3 us -> none  [advance(): squares - squared]
    pallas_call x0 -> x2, Pallas kernels: none -> 13.2 us  [the longest x1 10.7 us: shards(): pl.pallas_call(functools.partial(exchange, gy, gz), out_shape=jax.ShapeDt...]
    slice x12 -> x0, local copies, waits for them, and re-layouts: 6.22 us -> none  [the longest x6 4.75 us: padded_2(): lax.slice_in_dim(cells, cells.shape[dim] - width, cells.shape[dim], axis=...]
    ppermute x4 -> x0, local copies, waits for them, and re-layouts: 3.52 us -> none  [the longest x2 1.77 us: padded_2(): lax.ppermute(head, axis, [((i + 1) % count, i) for i in range(count)])]
    unnamed x13 -> x14, local copies, waits for them, and re-layouts: 0.12 us -> 2.8 us
    another operation x1 -> x0, local copies, waits for them, and re-layouts: 2.51 us -> none  [refine(): paired = jnp.stack([odd_cells, even_cells], axis=axis + 1)]
  transfers between devices with their start and end apart: 12 -> 0, of which waited for: 10 -> 0; matrix products, arithmetic and copies ran while one was open for 4% -> 0% of each run, Pallas kernels for 0% -> 0%
where the time goes in v1:
time: 16.3 us; the launch traced here: 16.1 us
  Pallas kernels  13.2 us (81%)
  local copies, waits for them, and re-layouts  2.8 us (17%)
    pallas_call x1, Pallas kernels, shards(): pl.pallas_call(functools.partial(exchange, gy, gz), out_shape=jax.ShapeDt...  10.7 us
    unnamed x14, local copies, waits for them, and re-layouts  2.8 us
    pallas_call x1, Pallas kernels, shards(): pl.pallas_call(relax, out_shape=jax.ShapeDtypeStruct((phases, 2, 2 * ny,...  2.56 us

profile of v1, /device:TPU:0, one launch (start us, length us, event | category | flops | bytes accessed | tf_op | source)
XLA Modules:
  0.0 16.1 jit_solution(12583999632686832356)
XLA Ops:
  0.0 0.0 copy-start.5
  0.0 0.0 copy-start.3
  0.0 0.0 copy-start
  0.0 0.0 copy-start.6
  0.0 10.7 %exchange.1.got = f32[19,8,128]{2,1,0:T(8,128)} custom-call(f32[8,1,32,64]{3,2,1,0:T(8,128)} %coarse_ref.3, s32[2,64,128]{2,1,0:T(8,128)} %labels_ref.3), custom_call_target="tpu_custom_call" | custom-call | tf_op jit(solution)/shard_map/exchange/pallas_call | solution.py:274
  10.7 0.0 copy-done.5
  10.7 0.0 copy-done.3
  10.7 0.0 copy-done
  10.7 0.0 copy-done.6
  10.7 0.0 copy-start.1
  10.7 1.0 %copy-done.1 = bf16[384,512]{1,0:T(8,128)(2,1)S(1)} copy-done((bf16[384,512]{1,0:T(8,128)(2,1)S(1)}, bf16[384,512]{1,0:T(8,128)(2,1)}, u32[]{:S(2)}) %copy-start.1) | copy-done | bytes 393240
  11.7 0.0 copy-start.2
  11.7 0.9 %copy-done.2 = f32[19,8,128]{2,1,0:T(8,128)S(1)} copy-done((f32[19,8,128]{2,1,0:T(8,128)S(1)}, f32[19,8,128]{2,1,0:T(8,128)}, u32[]{:S(2)}) %copy-start.2) | copy-done | bytes 77848
  12.6 0.0 copy-start.4
  12.6 0.9 %copy-done.4 = bf16[256,256]{1,0:T(8,128)(2,1)S(1)} copy-done((bf16[256,256]{1,0:T(8,128)(2,1)S(1)}, bf16[256,256]{1,0:T(8,128)(2,1)}, u32[]{:S(2)}) %copy-start.4) | copy-done | bytes 131096
  13.5 2.6 %relax.1 = f32[8,2,64,128]{3,2,1,0:T(8,128)} custom-call(f32[8,1,32,64]{3,2,1,0:T(8,128)S(1)} %copy-done, s32[2,64,128]{2,1,0:T(8,128)S(1)} %copy-done.3, f32[8]{0:T(128)S(1)} %copy-done.6, f32[19,8,128]{2,1,0:T(8,128)S(1)} %copy-done.2, bf16[128,128]{1,0:T(8,128)(2,1)S(1)} %copy-done.5, bf16[384,512]{1,0:T(8,128)(2,1)S(1)} %copy-done.1, ...), custom_call_target="tpu_custom_call" | custom-call | tf_op jit(solution)/shard_map/relax/pallas_call | solution.py:291
Async XLA Ops:
  0.0 10.7 %copy-start.5 = (bf16[128,128]{1,0:T(8,128)(2,1)S(1)}, bf16[128,128]{1,0:T(8,128)(2,1)}, u32[]{:S(2)}) copy-start(bf16[128,128]{1,0:T(8,128)(2,1)} %constant.6.clone.main_ref) | copy-start | bytes 98308
  0.0 10.7 %copy-start.3 = (s32[2,64,128]{2,1,0:T(8,128)S(1)}, s32[2,64,128]{2,1,0:T(8,128)}, u32[]{:S(2)}) copy-start(s32[2,64,128]{2,1,0:T(8,128)} %labels_ref.3) | copy-start | bytes 196612
  0.0 10.7 %copy-start = (f32[8,1,32,64]{3,2,1,0:T(8,128)S(1)}, f32[8,1,32,64]{3,2,1,0:T(8,128)}, u32[]{:S(2)}) copy-start(f32[8,1,32,64]{3,2,1,0:T(8,128)} %coarse_ref.3) | copy-start | bytes 196612
  0.0 10.7 %copy-start.6 = (f32[8]{0:T(128)S(1)}, f32[8]{0:T(128)}, u32[]{:S(2)}) copy-start(f32[8]{0:T(128)} %mobility_ref.1) | copy-start | bytes 100
  10.7 1.0 %copy-start.1 = (bf16[384,512]{1,0:T(8,128)(2,1)S(1)}, bf16[384,512]{1,0:T(8,128)(2,1)}, u32[]{:S(2)}) copy-start(bf16[384,512]{1,0:T(8,128)(2,1)} %constant.7.clone.strip_ref) | copy-start | bytes 1179652
  11.7 0.9 %copy-start.2 = (f32[19,8,128]{2,1,0:T(8,128)S(1)}, f32[19,8,128]{2,1,0:T(8,128)}, u32[]{:S(2)}) copy-start(f32[19,8,128]{2,1,0:T(8,128)} %exchange.1.got) | copy-start | bytes 233476
  12.6 0.9 %copy-start.4 = (bf16[256,256]{1,0:T(8,128)(2,1)S(1)}, bf16[256,256]{1,0:T(8,128)(2,1)}, u32[]{:S(2)}) copy-start(bf16[256,256]{1,0:T(8,128)(2,1)} %constant.8.clone.label_ref) | copy-start | bytes 393220

commit v2 on v1

--- a/solution.py
+++ b/solution.py
@@ -96,7 +96,9 @@
     return jnp.concatenate([x, jnp.zeros_like(x)], axis=-1)
 
 
-def exchange(gy, gz, coarse_ref, labels_ref, out_ref, stage, send_sem, recv_sem):
+def exchange(
+    gy, gz, coarse_hbm, labels_hbm, out_ref, coarse_ref, labels_ref, stage, send_sem, recv_sem, load_sem
+):
     me_y, me_z = lax.axis_index("gy"), lax.axis_index("gz")
 
     def other(dy, dz):
@@ -105,6 +107,14 @@
     barrier = pltpu.get_barrier_semaphore()
     for (dy, dz), _, _ in PARTS:
         pl.semaphore_signal(barrier, inc=1, device_id=other(dy, dz), device_id_type=MESH)
+    loads = [
+        pltpu.make_async_copy(coarse_hbm, coarse_ref, load_sem.at[0]),
+        pltpu.make_async_copy(labels_hbm, labels_ref, load_sem.at[1]),
+    ]
+    for load in loads:
+        load.start()
+    for load in loads:
+        load.wait()
 
     phases, _, ny, nz = coarse_ref.shape
     width = 2 * nz
@@ -274,14 +284,19 @@
     got = pl.pallas_call(
         functools.partial(exchange, gy, gz),
         out_shape=jax.ShapeDtypeStruct((SLOTS, phases, width), F32),
-        in_specs=[vmem] * 2,
+        in_specs=[pl.BlockSpec(memory_space=pltpu.HBM)] * 2,
         out_specs=vmem,
         scratch_shapes=[
+            pltpu.VMEM(coarse.shape, F32),
+            pltpu.VMEM(labels.shape, jnp.int32),
             pltpu.VMEM((10, phases, width), F32),
             pltpu.SemaphoreType.DMA((len(PARTS),)),
             pltpu.SemaphoreType.DMA((len(PARTS),)),
+            pltpu.SemaphoreType.DMA((2,)),
         ],
-        compiler_params=pltpu.CompilerParams(collective_id=0, has_side_effects=True),
+        compiler_params=pltpu.CompilerParams(
+            collective_id=0, has_side_effects=True, vmem_limit_bytes=4 * 2**20
+        ),
         name="exchange",
     )(coarse, labels)
     weights = [
@@ -294,7 +309,7 @@
         in_specs=[vmem] * 2 + [pl.BlockSpec(memory_space=pltpu.SMEM)] + [vmem] * 4,
         out_specs=vmem,
         scratch_shapes=[pltpu.VMEM((2, 2 * ny + 2, phases, width), F32)],
-        compiler_params=pltpu.CompilerParams(vmem_limit_bytes=16 * 2**20),
+        compiler_params=pltpu.CompilerParams(vmem_limit_bytes=8 * 2**20),
         name="relax",
     )(coarse, labels, mobility, got, *weights)
 

time: 16.3 us -> 15.5 us (0.951)
  Pallas kernels: 13.2 us -> 11.6 us
  local copies, waits for them, and re-layouts: 2.8 us -> 3.5 us
    pallas_call x1, Pallas kernels: 10.7 us -> 9.08 us  [shards(): pl.pallas_call(functools.partial(exchange, gy, gz), out_shape=jax.ShapeDt...]
    unnamed x14, local copies, waits for them, and re-layouts: 2.8 us -> 3.5 us
where the time goes in v2:
time: 15.5 us; the launch traced here: 15.2 us
  Pallas kernels  11.6 us (75%)
  local copies, waits for them, and re-layouts  3.5 us (23%)
    pallas_call x1, Pallas kernels, shards(): pl.pallas_call(functools.partial(exchange, gy, gz), out_shape=jax.ShapeDt...  9.08 us
    unnamed x14, local copies, waits for them, and re-layouts  3.5 us
    pallas_call x1, Pallas kernels, shards(): pl.pallas_call(relax, out_shape=jax.ShapeDtypeStruct((phases, 2, 2 * ny,...  2.56 us

profile of v2, /device:TPU:0, one launch (start us, length us, event | category | flops | bytes accessed | tf_op | source)
XLA Modules:
  0.0 15.2 jit_solution(11956248622613082585)
XLA Ops:
  0.0 0.0 copy-start
  0.0 0.9 %copy-done = f32[8,1,32,64]{3,2,1,0:T(8,128)S(1)} copy-done((f32[8,1,32,64]{3,2,1,0:T(8,128)S(1)}, f32[8,1,32,64]{3,2,1,0:T(8,128)}, u32[]{:S(2)}) %copy-start) | copy-done | bytes 65560
  0.9 0.0 copy-start.3
  0.9 0.8 %copy-done.3 = s32[2,64,128]{2,1,0:T(8,128)S(1)} copy-done((s32[2,64,128]{2,1,0:T(8,128)S(1)}, s32[2,64,128]{2,1,0:T(8,128)}, u32[]{:S(2)}) %copy-start.3) | copy-done | bytes 65560
  1.7 0.0 copy-start.1
  1.7 0.0 copy-start.4
  1.7 0.0 copy-start.6
  1.8 9.1 %exchange.1.got = f32[19,8,128]{2,1,0:T(8,128)S(1)} custom-call(f32[8,1,32,64]{3,2,1,0:T(8,128)S(1)} %copy-done, s32[2,64,128]{2,1,0:T(8,128)S(1)} %copy-done.3), custom_call_target="tpu_custom_call" | custom-call | tf_op jit(solution)/shard_map/exchange/pallas_call | solution.py:284
  10.8 0.0 copy-done.1
  10.8 0.0 copy-done.4
  10.9 0.0 copy-done.6
  10.9 0.0 copy-start.2
  10.9 1.0 %copy-done.2 = bf16[384,512]{1,0:T(8,128)(2,1)S(1)} copy-done((bf16[384,512]{1,0:T(8,128)(2,1)S(1)}, bf16[384,512]{1,0:T(8,128)(2,1)}, u32[]{:S(2)}) %copy-start.2) | copy-done | bytes 393240
  11.9 0.0 copy-start.5
  11.9 0.8 %copy-done.5 = bf16[128,128]{1,0:T(8,128)(2,1)S(1)} copy-done((bf16[128,128]{1,0:T(8,128)(2,1)S(1)}, bf16[128,128]{1,0:T(8,128)(2,1)}, u32[]{:S(2)}) %copy-start.5) | copy-done | bytes 32792
  12.6 2.6 %relax.1 = f32[8,2,64,128]{3,2,1,0:T(8,128)} custom-call(f32[8,1,32,64]{3,2,1,0:T(8,128)S(1)} %copy-done.1, s32[2,64,128]{2,1,0:T(8,128)S(1)} %copy-done.3, f32[8]{0:T(128)S(1)} %copy-done.6, f32[19,8,128]{2,1,0:T(8,128)S(1)} %exchange.1.got, bf16[128,128]{1,0:T(8,128)(2,1)S(1)} %copy-done.5, bf16[384,512]{1,0:T(8,128)(2,1)S(1)} %copy-done.2, ...), custom_call_target="tpu_custom_call" | custom-call | tf_op jit(solution)/shard_map/relax/pallas_call | solution.py:306
Async XLA Ops:
  0.0 0.9 %copy-start = (f32[8,1,32,64]{3,2,1,0:T(8,128)S(1)}, f32[8,1,32,64]{3,2,1,0:T(8,128)}, u32[]{:S(2)}) copy-start(f32[8,1,32,64]{3,2,1,0:T(8,128)} %coarse_ref.1) | copy-start | bytes 196612
  0.9 0.8 %copy-start.3 = (s32[2,64,128]{2,1,0:T(8,128)S(1)}, s32[2,64,128]{2,1,0:T(8,128)}, u32[]{:S(2)}) copy-start(s32[2,64,128]{2,1,0:T(8,128)} %labels_ref.1) | copy-start | bytes 196612
  1.7 9.1 %copy-start.1 = (f32[8,1,32,64]{3,2,1,0:T(8,128)S(1)}, f32[8,1,32,64]{3,2,1,0:T(8,128)}, u32[]{:S(2)}) copy-start(f32[8,1,32,64]{3,2,1,0:T(8,128)} %coarse_ref.1) | copy-start | bytes 196612
  1.7 9.1 %copy-start.4 = (bf16[256,256]{1,0:T(8,128)(2,1)S(1)}, bf16[256,256]{1,0:T(8,128)(2,1)}, u32[]{:S(2)}) copy-start(bf16[256,256]{1,0:T(8,128)(2,1)} %constant.8.clone.label_ref) | copy-start | bytes 393220
  1.7 9.1 %copy-start.6 = (f32[8]{0:T(128)S(1)}, f32[8]{0:T(128)}, u32[]{:S(2)}) copy-start(f32[8]{0:T(128)} %mobility_ref.1) | copy-start | bytes 100
  10.9 1.0 %copy-start.2 = (bf16[384,512]{1,0:T(8,128)(2,1)S(1)}, bf16[384,512]{1,0:T(8,128)(2,1)}, u32[]{:S(2)}) copy-start(bf16[384,512]{1,0:T(8,128)(2,1)} %constant.7.clone.strip_ref) | copy-start | bytes 1179652
  11.9 0.8 %copy-start.5 = (bf16[128,128]{1,0:T(8,128)(2,1)S(1)}, bf16[128,128]{1,0:T(8,128)(2,1)}, u32[]{:S(2)}) copy-start(bf16[128,128]{1,0:T(8,128)(2,1)} %constant.6.clone.main_ref) | copy-start | bytes 98308

commit v3 on v1

--- a/solution.py
+++ b/solution.py
@@ -89,14 +89,23 @@
     ((1, -1), (3, 5), (14, 16)),
     ((1, 1), (3, 5), (16, 18)),
 )
-SLOTS = 19
+SLOTS = 21
 
 
 def wide(x):
     return jnp.concatenate([x, jnp.zeros_like(x)], axis=-1)
 
 
-def exchange(gy, gz, coarse_ref, labels_ref, out_ref, stage, send_sem, recv_sem):
+def exact_dot(x, w):
+    high = x.astype(BF16)
+    low = (x - high.astype(F32)).astype(BF16)
+    return jnp.dot(high, w, preferred_element_type=F32) + jnp.dot(low, w, preferred_element_type=F32)
+
+
+def exchange(gy, gz, *refs):
+    mobility_ref, sources, refs = refs[0], refs[1:6], refs[6:]
+    got, fine_ref, rate_ref, labels_ref, main_ref, strip_ref, label_ref = refs[:7]
+    coarse_ref, stage, send_sem, recv_sem, load_sem = refs[7:]
     me_y, me_z = lax.axis_index("gy"), lax.axis_index("gz")
 
     def other(dy, dz):
@@ -105,12 +114,24 @@
     barrier = pltpu.get_barrier_semaphore()
     for (dy, dz), _, _ in PARTS:
         pl.semaphore_signal(barrier, inc=1, device_id=other(dy, dz), device_id_type=MESH)
+    targets = (coarse_ref, labels_ref, main_ref, strip_ref, label_ref)
+    loads = [
+        pltpu.make_async_copy(source, target, load_sem.at[n])
+        for n, (source, target) in enumerate(zip(sources, targets))
+    ]
+    for load in loads:
+        load.start()
 
     phases, _, ny, nz = coarse_ref.shape
     width = 2 * nz
-    x = jnp.swapaxes(coarse_ref[:, 0], 0, 1)
-    rows = [wide(x[r]) for r in range(ny)]
     lane = lax.broadcasted_iota(jnp.int32, (phases, width), 1)
+    loads[0].wait()
+    x = wide(jnp.swapaxes(coarse_ref[:, 0], 0, 1))
+    rows = [x[r] for r in range(ny)]
+    stage[0] = rows[0]
+    stage[1] = rows[1]
+    stage[3] = rows[ny - 2]
+    stage[4] = rows[ny - 1]
     left = jnp.zeros((phases, width), F32)
     right = jnp.zeros((phases, width), F32)
     for r in range(ny):
@@ -119,35 +140,32 @@
         low = nz - 2 + 2 * r
         right = jnp.where((lane >= low) & (lane < low + 2), turned, right)
     right = pltpu.roll(right, (2 * ny - (nz - 2)) % width, 1)
-
-    labels = labels_ref[...].astype(F32)
-    flat = labels.reshape(-1, width)
-    pick_lane = lax.broadcasted_iota(jnp.int32, (phases, width), 1)
+    stage[6] = left
+    stage[8] = right
+    got[SLOTS - 3] = rows[0]
+    got[SLOTS - 2] = rows[ny - 1]
+    got[SLOTS - 1] = left + right
+
+    loads[1].wait()
+    flat = labels_ref[...].reshape(-1, width).astype(F32).astype(BF16)
 
     def column(z):
-        pick = (pick_lane == z).astype(BF16)
+        pick = (lane == z).astype(BF16)
         return lax.dot_general(
-            pick, flat.astype(BF16), (((1,), (1,)), ((), ())), preferred_element_type=F32
+            pick, flat, (((1,), (1,)), ((), ())), preferred_element_type=F32
         )
 
-    stage[0] = rows[0]
-    stage[1] = rows[1]
-    stage[2, 0:2] = labels[:, 0]
-    stage[3] = rows[ny - 2]
-    stage[4] = rows[ny - 1]
-    stage[5, 0:2] = labels[:, 2 * ny - 1]
-    stage[6] = left
+    stage[2, 0:2] = labels_ref[:, 0].astype(F32)
+    stage[5, 0:2] = labels_ref[:, 2 * ny - 1].astype(F32)
     stage[7] = column(0)
-    stage[8] = right
     stage[9] = column(width - 1)
-    out_ref[SLOTS - 1] = left + right
 
     pl.semaphore_wait(barrier, len(PARTS))
     copies = []
     for n, ((dy, dz), (s0, s1), (d0, d1)) in enumerate(PARTS):
         copy = pltpu.make_async_remote_copy(
             src_ref=stage.at[s0:s1],
-            dst_ref=out_ref.at[d0:d1],
+            dst_ref=got.at[d0:d1],
             send_sem=send_sem.at[n],
             recv_sem=recv_sem.at[n],
             device_id=other(dy, dz),
@@ -155,27 +173,30 @@
         )
         copy.start()
         copies.append(copy)
+
+    phase_id = lax.broadcasted_iota(jnp.int32, (phases, width), 0)
+    rate = jnp.zeros((phases, width), F32)
+    for p in range(phases):
+        rate = jnp.where(phase_id == p, STEP * mobility_ref[p], rate)
+    rate_ref[...] = rate
+    loads[2].wait()
+    fine_ref[...] = exact_dot(x.reshape(-1, width), main_ref[...]).reshape(fine_ref.shape)
+    for load in loads[3:]:
+        load.wait()
     for copy in copies:
         copy.wait()
 
 
-def exact_dot(x, w):
-    high = x.astype(BF16)
-    low = (x - high.astype(F32)).astype(BF16)
-    return jnp.dot(high, w, preferred_element_type=F32) + jnp.dot(low, w, preferred_element_type=F32)
-
-
-def relax(coarse_ref, labels_ref, mobility_ref, got, main_ref, strip_ref, label_ref, out_ref, p1):
-    phases, _, ny, nz = coarse_ref.shape
-    width = 2 * nz
-    fy = 2 * ny
+def relax(
+    got, own, rate_ref, labels_ref, main_ref, strip_ref, label_ref, out_hbm, p1, out_ref, out_sem
+):
+    ny, phases, width = own.shape
+    nz, fy = width // 2, 2 * ny
     shape = (phases, width)
     lane = lax.broadcasted_iota(jnp.int32, shape, 1)
     phase_id = lax.broadcasted_iota(jnp.int32, shape, 0)
     phase_f = phase_id.astype(F32)
-    rate = jnp.zeros(shape, F32)
-    for p in range(phases):
-        rate = jnp.where(phase_id == p, STEP * mobility_ref[p], rate)
+    rate = rate_ref[...]
     first, last = lane == 0, lane == width - 1
     ends = first | last
 
@@ -197,15 +218,13 @@
 
     below = [edge(got[n], got[12 + n], got[10 + n]) for n in range(2)]
     above = [edge(got[3 + n], got[16 + n], got[14 + n]) for n in range(2)]
-    x = jnp.swapaxes(coarse_ref[:, 0], 0, 1)
-    x = jnp.concatenate([x, jnp.zeros_like(x)], axis=-1)
-    top = edge(x[0], got[8], got[6], width - 2 - 2 * ny, nz)
     low = 2 * (ny - 1)
-    bottom = edge(x[ny - 1], got[8], got[6], width - 2 - 2 * ny - low, nz - low)
-    rows = jnp.concatenate(
-        [jnp.stack([*above, top]), x[1 : ny - 1], jnp.stack([bottom, *below])], axis=0
-    )
-    fine_z = exact_dot(rows.reshape(-1, width), main_ref[...]).reshape(ny + 4, phases, width)
+    top = edge(got[SLOTS - 3], got[8], got[6], width - 2 - 2 * ny, nz)
+    bottom = edge(got[SLOTS - 2], got[8], got[6], width - 2 - 2 * ny - low, nz - low)
+    rim_rows = jnp.concatenate([*above, top, bottom, *below], axis=0)
+    rim_fine = exact_dot(rim_rows, main_ref[...])
+    rim_fine = [rim_fine[n * phases : (n + 1) * phases] for n in range(6)]
+    fine_z = [*rim_fine[:3], *(own[r] for r in range(1, ny - 1)), *rim_fine[3:]]
 
     beside = jnp.where(lane < 2 * ny, got[6], got[8])
     near = (lane < 4) | (lane >= nz - 4) & (lane < nz + 4) | (lane >= width - 4)
@@ -239,9 +258,7 @@
     def pinned(n, y):
         return jnp.where(label_row(n, y), rate, 0.0)
 
-    prev, cur = fine_row(-2), fine_row(-1)
-    for y in range(-1, fy + 1):
-        nxt = fine_row(y + 1)
+    def first_step(y, prev, cur, nxt):
         if y < 0:
             beside_row = corner
         elif y == fy:
@@ -251,9 +268,8 @@
         base = cur + rate * (prev + nxt + around(cur, beside_row) - cur * (4.0 + total(cur)))
         for n in range(2):
             p1[n, y + 1] = base + pinned(n, y)
-        prev, cur = cur, nxt
-
-    for block in range(fy // 8):
+
+    def second_step(block):
         done = [[], []]
         for y in range(8 * block, 8 * block + 8):
             both = [p1[n, y + 1] for n in range(2)]
@@ -263,7 +279,23 @@
                 near = near + 2.0 * both[1 - n]
                 done[n].append(c + rate * (near - c * (6.0 + total(c))) + pinned(n, y))
         for n in range(2):
-            out_ref[:, n, 8 * block : 8 * block + 8] = jnp.swapaxes(jnp.stack(done[n]), 0, 1)
+            out_ref[block, :, n] = jnp.swapaxes(jnp.stack(done[n]), 0, 1)
+        copy = pltpu.make_async_copy(
+            out_ref.at[block], out_hbm.at[:, :, pl.ds(8 * block, 8)], out_sem.at[block]
+        )
+        copy.start()
+        return copy
+
+    copies = []
+    prev, cur = fine_row(-2), fine_row(-1)
+    for y in range(-1, fy + 1):
+        nxt = fine_row(y + 1)
+        first_step(y, prev, cur, nxt)
+        prev, cur = cur, nxt
+        if y > 0 and y % 8 == 0:
+            copies.append(second_step(y // 8 - 1))
+    for copy in copies:
+        copy.wait()
 
 
 def shards(gy, gz, coarse, labels, mobility):
@@ -271,32 +303,48 @@
     assert planes == 1 and labels.shape == (2, 2 * ny, 2 * nz) and ny <= nz // 2 and phases == 8
     width = 2 * nz
     vmem = pl.BlockSpec(memory_space=pltpu.VMEM)
-    got = pl.pallas_call(
-        functools.partial(exchange, gy, gz),
-        out_shape=jax.ShapeDtypeStruct((SLOTS, phases, width), F32),
-        in_specs=[vmem] * 2,
-        out_specs=vmem,
-        scratch_shapes=[
-            pltpu.VMEM((10, phases, width), F32),
-            pltpu.SemaphoreType.DMA((len(PARTS),)),
-            pltpu.SemaphoreType.DMA((len(PARTS),)),
-        ],
-        compiler_params=pltpu.CompilerParams(collective_id=0, has_side_effects=True),
-        name="exchange",
-    )(coarse, labels)
+    hbm = pl.BlockSpec(memory_space=pltpu.HBM)
     weights = [
         jnp.asarray(w, BF16)
         for w in (main_operator(nz), strip_operator(ny, nz), label_operator(ny, nz))
     ]
+    sources = [pltpu.with_memory_space_constraint(v, pltpu.HBM) for v in (coarse, labels, *weights)]
+    shared = [
+        pltpu.VMEM((SLOTS, phases, width), F32),
+        pltpu.VMEM((ny, phases, width), F32),
+        pltpu.VMEM((phases, width), F32),
+        *(pltpu.VMEM(v.shape, v.dtype) for v in (labels, *weights)),
+    ]
+    parts = pl.pallas_call(
+        functools.partial(exchange, gy, gz),
+        out_shape=shared,
+        in_specs=[pl.BlockSpec(memory_space=pltpu.SMEM)] + [hbm] * len(sources),
+        out_specs=[vmem] * len(shared),
+        scratch_shapes=[
+            pltpu.VMEM(coarse.shape, F32),
+            pltpu.VMEM((10, phases, width), F32),
+            pltpu.SemaphoreType.DMA((len(PARTS),)),
+            pltpu.SemaphoreType.DMA((len(PARTS),)),
+            pltpu.SemaphoreType.DMA((len(sources),)),
+        ],
+        compiler_params=pltpu.CompilerParams(
+            collective_id=0, has_side_effects=True, vmem_limit_bytes=8 * 2**20
+        ),
+        name="exchange",
+    )(mobility, *sources)
     return pl.pallas_call(
         relax,
         out_shape=jax.ShapeDtypeStruct((phases, 2, 2 * ny, width), F32),
-        in_specs=[vmem] * 2 + [pl.BlockSpec(memory_space=pltpu.SMEM)] + [vmem] * 4,
-        out_specs=vmem,
-        scratch_shapes=[pltpu.VMEM((2, 2 * ny + 2, phases, width), F32)],
-        compiler_params=pltpu.CompilerParams(vmem_limit_bytes=16 * 2**20),
+        in_specs=[vmem] * len(shared),
+        out_specs=hbm,
+        scratch_shapes=[
+            pltpu.VMEM((2, 2 * ny + 2, phases, width), F32),
+            pltpu.VMEM((2 * ny // 8, phases, 2, 8, width), F32),
+            pltpu.SemaphoreType.DMA((2 * ny // 8,)),
+        ],
+        compiler_params=pltpu.CompilerParams(vmem_limit_bytes=8 * 2**20),
         name="relax",
-    )(coarse, labels, mobility, got, *weights)
+    )(*parts)
 
 
 def solution(mesh):

time: 16.3 us -> 13.3 us (0.82)
  local copies, waits for them, and re-layouts: 2.8 us -> 0.65 us
  Pallas kernels: 13.2 us -> 12.5 us
    unnamed x14 -> x2, local copies, waits for them, and re-layouts: 2.8 us -> 0.65 us
    pallas_call x1, Pallas kernels: 10.7 us -> 10.2 us  [shards(): pl.pallas_call(functools.partial(exchange, gy, gz), out_shape=shared, in_...]
    pallas_call x1, Pallas kernels: 2.56 us -> 2.3 us  [shards(): pl.pallas_call(relax, out_shape=jax.ShapeDtypeStruct((phases, 2, 2 * ny,...]
where the time goes in v3:
time: 13.3 us; the launch traced here: 13.2 us
  Pallas kernels  12.5 us (94%)
  local copies, waits for them, and re-layouts  0.65 us (5%)
    pallas_call x1, Pallas kernels, shards(): pl.pallas_call(functools.partial(exchange, gy, gz), out_shape=shared, in_...  10.2 us
    pallas_call x1, Pallas kernels, shards(): pl.pallas_call(relax, out_shape=jax.ShapeDtypeStruct((phases, 2, 2 * ny,...  2.3 us
    unnamed x2, local copies, waits for them, and re-layouts  0.65 us

profile of v3, /device:TPU:0, one launch (start us, length us, event | category | flops | bytes accessed | tf_op | source)
XLA Modules:
  0.0 13.2 jit_solution(13439373250427739958)
XLA Ops:
  0.0 0.0 copy-start
  0.0 0.7 %copy-done = f32[8]{0:T(128)S(1)} copy-done((f32[8]{0:T(128)S(1)}, f32[8]{0:T(128)}, u32[]{:S(2)}) %copy-start) | copy-done | bytes 56
  0.7 10.2 %exchange.1 = (f32[21,8,128]{2,1,0:T(8,128)S(1)}, f32[32,8,128]{2,1,0:T(8,128)S(1)}, f32[8,128]{1,0:T(8,128)S(1)}, s32[2,64,128]{2,1,0:T(8,128)S(1)}, bf16[128,1...) custom-call(f32[8]{0:T(128)S(1)} %copy-done, f32[8,1,32,64]{3,2,1,0:T(8,128)} %refs_1_.1, ...), custom_call_target="tpu_custom_call" | custom-call | tf_op jit(solution)/shard_map/exchange/pallas_call | solution.py:318
  10.9 2.3 %relax.1 = f32[8,2,64,128]{3,2,1,0:T(8,128)} custom-call(f32[21,8,128]{2,1,0:T(8,128)S(1)} %get-tuple-element.12.got, f32[32,8,128]{2,1,0:T(8,128)S(1)} %get-tuple-element.13.own, f32[8,128]{1,0:T(8,128)S(1)} %get-tuple-element.14.rate_ref, s32[2,64,128]{2,1,0:T(8,128)S(1)} %get-tuple-element.15.labels_ref, bf16[128,128]{1,0:T(8,128)(2,1)S(1)} %get-tuple-element.16.main_ref, ...), custom_call_target="tpu_custom_call" | custom-call | tf_op jit(solution)/shard_map/relax/pallas_call | solution.py:335
Async XLA Ops:
  0.0 0.7 %copy-start = (f32[8]{0:T(128)S(1)}, f32[8]{0:T(128)}, u32[]{:S(2)}) copy-start(f32[8]{0:T(128)} %refs_0_.1) | copy-start | bytes 100

commit v4 on v3

--- a/solution.py
+++ b/solution.py
@@ -89,7 +89,7 @@
     ((1, -1), (3, 5), (14, 16)),
     ((1, 1), (3, 5), (16, 18)),
 )
-SLOTS = 21
+SLOTS = 20
 
 
 def wide(x):
@@ -97,15 +97,16 @@
 
 
 def exact_dot(x, w):
-    high = x.astype(BF16)
-    low = (x - high.astype(F32)).astype(BF16)
-    return jnp.dot(high, w, preferred_element_type=F32) + jnp.dot(low, w, preferred_element_type=F32)
+    high = x.astype(BF16).astype(F32)
+    both = jnp.concatenate([high, x - high], axis=0).astype(BF16)
+    product = jnp.dot(both, w, preferred_element_type=F32)
+    return product[: x.shape[0]] + product[x.shape[0] :]
 
 
 def exchange(gy, gz, *refs):
-    mobility_ref, sources, refs = refs[0], refs[1:6], refs[6:]
-    got, fine_ref, rate_ref, labels_ref, main_ref, strip_ref, label_ref = refs[:7]
-    coarse_ref, stage, send_sem, recv_sem, load_sem = refs[7:]
+    sources, refs = refs[:6], refs[6:]
+    got, fine_ref, pin_ref, rate_ref, strips_ref, main_ref, strip_ref, label_ref = refs[:8]
+    mobility_ref, labels_ref, coarse_ref, stage, send_sem, recv_sem, load_sem = refs[8:]
     me_y, me_z = lax.axis_index("gy"), lax.axis_index("gz")
 
     def other(dy, dz):
@@ -114,7 +115,7 @@
     barrier = pltpu.get_barrier_semaphore()
     for (dy, dz), _, _ in PARTS:
         pl.semaphore_signal(barrier, inc=1, device_id=other(dy, dz), device_id_type=MESH)
-    targets = (coarse_ref, labels_ref, main_ref, strip_ref, label_ref)
+    targets = (coarse_ref, labels_ref, mobility_ref, main_ref, strip_ref, label_ref)
     loads = [
         pltpu.make_async_copy(source, target, load_sem.at[n])
         for n, (source, target) in enumerate(zip(sources, targets))
@@ -142,9 +143,8 @@
     right = pltpu.roll(right, (2 * ny - (nz - 2)) % width, 1)
     stage[6] = left
     stage[8] = right
-    got[SLOTS - 3] = rows[0]
-    got[SLOTS - 2] = rows[ny - 1]
-    got[SLOTS - 1] = left + right
+    got[SLOTS - 2] = rows[0]
+    got[SLOTS - 1] = rows[ny - 1]
 
     loads[1].wait()
     flat = labels_ref[...].reshape(-1, width).astype(F32).astype(BF16)
@@ -176,22 +176,32 @@
 
     phase_id = lax.broadcasted_iota(jnp.int32, (phases, width), 0)
     rate = jnp.zeros((phases, width), F32)
+    loads[2].wait()
     for p in range(phases):
         rate = jnp.where(phase_id == p, STEP * mobility_ref[p], rate)
     rate_ref[...] = rate
-    loads[2].wait()
-    fine_ref[...] = exact_dot(x.reshape(-1, width), main_ref[...]).reshape(fine_ref.shape)
-    for load in loads[3:]:
-        load.wait()
+    loads[3].wait()
+    fine_z = exact_dot(x.reshape(-1, width), main_ref[...]).reshape(ny, phases, width)
+    for y in range(1, 2 * ny - 1):
+        (r0, a), (r1, b) = taps(y)
+        fine_ref[y] = a * fine_z[r0] + b * fine_z[r1]
+    for n in range(2):
+        for y in range(2 * ny):
+            label = jnp.broadcast_to(labels_ref[n, y : y + 1], rate.shape)
+            pin_ref[n, y] = jnp.where(label == phase_id, rate, 0.0)
+    loads[4].wait()
+    strips_ref[...] = exact_dot(left + right, strip_ref[:width])
+    loads[5].wait()
     for copy in copies:
         copy.wait()
 
 
 def relax(
-    got, own, rate_ref, labels_ref, main_ref, strip_ref, label_ref, out_hbm, p1, out_ref, out_sem
+    got, fine, pin, rate_ref, strips_ref, main_ref, strip_ref, label_ref, *rest
 ):
-    ny, phases, width = own.shape
-    nz, fy = width // 2, 2 * ny
+    out_hbm, p1, out_ref, out_sem = rest
+    fy, phases, width = fine.shape
+    ny, nz = fy // 2, width // 2
     shape = (phases, width)
     lane = lax.broadcasted_iota(jnp.int32, shape, 1)
     phase_id = lax.broadcasted_iota(jnp.int32, shape, 0)
@@ -219,17 +229,18 @@
     below = [edge(got[n], got[12 + n], got[10 + n]) for n in range(2)]
     above = [edge(got[3 + n], got[16 + n], got[14 + n]) for n in range(2)]
     low = 2 * (ny - 1)
-    top = edge(got[SLOTS - 3], got[8], got[6], width - 2 - 2 * ny, nz)
-    bottom = edge(got[SLOTS - 2], got[8], got[6], width - 2 - 2 * ny - low, nz - low)
+    top = edge(got[SLOTS - 2], got[8], got[6], width - 2 - 2 * ny, nz)
+    bottom = edge(got[SLOTS - 1], got[8], got[6], width - 2 - 2 * ny - low, nz - low)
     rim_rows = jnp.concatenate([*above, top, bottom, *below], axis=0)
     rim_fine = exact_dot(rim_rows, main_ref[...])
     rim_fine = [rim_fine[n * phases : (n + 1) * phases] for n in range(6)]
-    fine_z = [*rim_fine[:3], *(own[r] for r in range(1, ny - 1)), *rim_fine[3:]]
+    at_rim = dict(zip((-2, -1, 0, ny - 1, ny, ny + 1), rim_fine))
 
     beside = jnp.where(lane < 2 * ny, got[6], got[8])
     near = (lane < 4) | (lane >= nz - 4) & (lane < nz + 4) | (lane >= width - 4)
     rim = jnp.where(near, above[1], turn(below[0], 8))
-    strips = exact_dot(jnp.concatenate([got[SLOTS - 1], beside, rim], axis=1), strip_ref[...])
+    strips = exact_dot(jnp.concatenate([beside, rim], axis=1), strip_ref[width:])
+    strips = strips + strips_ref[...]
     outer, side, inner, corner = (strips[:, n * width : (n + 1) * width] for n in range(4))
     near_labels = jnp.concatenate([got[9], got[7]], axis=1).astype(BF16)
     strip_labels = jnp.dot(near_labels, label_ref[...], preferred_element_type=F32)
@@ -242,21 +253,18 @@
     ]
 
     def fine_row(y):
-        (r0, a), (r1, b) = taps(y)
-        v = a * fine_z[r0 + 2] + b * fine_z[r1 + 2]
+        if 0 < y < fy - 1:
+            v = fine[y]
+        else:
+            (r0, a), (r1, b) = taps(y)
+            v = a * at_rim[r0] + b * at_rim[r1]
         return jnp.where(ends, turn(inner, -2 * y), v) if 0 <= y < fy else v
 
-    def label_row(n, y):
-        if y < 0:
-            row = got[5, n : n + 1]
-        elif y >= fy:
-            row = got[2, n : n + 1]
-        else:
-            return jnp.broadcast_to(labels_ref[n, y : y + 1], shape) == phase_id
-        return jnp.broadcast_to(row, shape) == phase_f
-
     def pinned(n, y):
-        return jnp.where(label_row(n, y), rate, 0.0)
+        if 0 <= y < fy:
+            return pin[n, y]
+        row = got[5, n : n + 1] if y < 0 else got[2, n : n + 1]
+        return jnp.where(jnp.broadcast_to(row, shape) == phase_f, rate, 0.0)
 
     def first_step(y, prev, cur, nxt):
         if y < 0:
@@ -308,19 +316,23 @@
         jnp.asarray(w, BF16)
         for w in (main_operator(nz), strip_operator(ny, nz), label_operator(ny, nz))
     ]
-    sources = [pltpu.with_memory_space_constraint(v, pltpu.HBM) for v in (coarse, labels, *weights)]
+    sources = [pltpu.with_memory_space_constraint(v, pltpu.HBM) for v in (coarse, labels, mobility, *weights)]
     shared = [
         pltpu.VMEM((SLOTS, phases, width), F32),
-        pltpu.VMEM((ny, phases, width), F32),
+        pltpu.VMEM((2 * ny, phases, width), F32),
+        pltpu.VMEM((2, 2 * ny, phases, width), F32),
         pltpu.VMEM((phases, width), F32),
-        *(pltpu.VMEM(v.shape, v.dtype) for v in (labels, *weights)),
+        pltpu.VMEM((phases, 4 * width), F32),
+        *(pltpu.VMEM(v.shape, v.dtype) for v in weights),
     ]
     parts = pl.pallas_call(
         functools.partial(exchange, gy, gz),
         out_shape=shared,
-        in_specs=[pl.BlockSpec(memory_space=pltpu.SMEM)] + [hbm] * len(sources),
+        in_specs=[hbm] * len(sources),
         out_specs=[vmem] * len(shared),
         scratch_shapes=[
+            pltpu.SMEM(mobility.shape, F32),
+            pltpu.VMEM(labels.shape, jnp.int32),
             pltpu.VMEM(coarse.shape, F32),
             pltpu.VMEM((10, phases, width), F32),
             pltpu.SemaphoreType.DMA((len(PARTS),)),
@@ -331,7 +343,7 @@
             collective_id=0, has_side_effects=True, vmem_limit_bytes=8 * 2**20
         ),
         name="exchange",
-    )(mobility, *sources)
+    )(*sources)
     return pl.pallas_call(
         relax,
         out_shape=jax.ShapeDtypeStruct((phases, 2, 2 * ny, width), F32),

time: 13.3 us -> 12 us (0.902)
  local copies, waits for them, and re-layouts: 0.65 us -> 0 us
  Pallas kernels: 12.5 us -> 11.9 us
    unnamed x2 -> x0, local copies, waits for them, and re-layouts: 0.65 us -> none
    pallas_call x1, Pallas kernels: 10.2 us -> 9.6 us  [shards(): pl.pallas_call(functools.partial(exchange, gy, gz), out_shape=shared, in_...]
where the time goes in v4:
time: 12 us; the launch traced here: 11.9 us
  Pallas kernels  11.9 us (99%)
    pallas_call x1, Pallas kernels, shards(): pl.pallas_call(functools.partial(exchange, gy, gz), out_shape=shared, in_...  9.6 us
    pallas_call x1, Pallas kernels, shards(): pl.pallas_call(relax, out_shape=jax.ShapeDtypeStruct((phases, 2, 2 * ny,...  2.28 us

profile of v4, /device:TPU:0, one launch (start us, length us, event | category | flops | bytes accessed | tf_op | source)
XLA Modules:
  0.0 11.9 jit_solution(18308562792422068261)
XLA Ops:
  0.0 9.6 %exchange.1 = (f32[20,8,128]{2,1,0:T(8,128)S(1)}, f32[64,8,128]{2,1,0:T(8,128)S(1)}, f32[2,64,8,128]{3,2,1,0:T(8,128)S(1)}, f32[8,128]{1,0:T(8,128)S(1)}, f32[8,...) custom-call(f32[8,1,32,64]{3,2,1,0:T(8,128)} %refs_0_.1, ...), custom_call_target="tpu_custom_call" | custom-call | tf_op jit(solution)/shard_map/exchange/pallas_call | solution.py:328
  9.6 2.3 %relax.1 = f32[8,2,64,128]{3,2,1,0:T(8,128)} custom-call(f32[20,8,128]{2,1,0:T(8,128)S(1)} %get-tuple-element.13.got, f32[64,8,128]{2,1,0:T(8,128)S(1)} %get-tuple-element.14.fine, f32[2,64,8,128]{3,2,1,0:T(8,128)S(1)} %get-tuple-element.15.pin, f32[8,128]{1,0:T(8,128)S(1)} %get-tuple-element.16.rate_ref, f32[8,512]{1,0:T(8,128)S(1)} %get-tuple-element.17.strips_ref, ...), custom_call_target="tpu_custom_call" | custom-call | tf_op jit(solution)/shard_map/relax/pallas_call | solution.py:347

commit v5 on v4

--- a/solution.py
+++ b/solution.py
@@ -105,8 +105,9 @@
 
 def exchange(gy, gz, *refs):
     sources, refs = refs[:6], refs[6:]
-    got, fine_ref, pin_ref, rate_ref, strips_ref, main_ref, strip_ref, label_ref = refs[:8]
-    mobility_ref, labels_ref, coarse_ref, stage, send_sem, recv_sem, load_sem = refs[8:]
+    got, fine_ref, pin_ref, rate_ref, strips_ref, beside_ref, ones_ref = refs[:7]
+    main_ref, strip_ref, label_ref = refs[7:10]
+    mobility_ref, labels_ref, coarse_ref, stage, send_sem, recv_sem, load_sem = refs[10:]
     me_y, me_z = lax.axis_index("gy"), lax.axis_index("gz")
 
     def other(dy, dz):
@@ -189,6 +190,12 @@
         for y in range(2 * ny):
             label = jnp.broadcast_to(labels_ref[n, y : y + 1], rate.shape)
             pin_ref[n, y] = jnp.where(label == phase_id, rate, 0.0)
+    row = lax.broadcasted_iota(jnp.int32, beside_ref.shape, 0) % width
+    column_id = lax.broadcasted_iota(jnp.int32, beside_ref.shape, 1)
+    beside_ref[...] = (jnp.abs(row - column_id) == 1).astype(F32).astype(BF16)
+    row = lax.broadcasted_iota(jnp.int32, ones_ref.shape, 0)
+    column_id = lax.broadcasted_iota(jnp.int32, ones_ref.shape, 1) % (8 * phases)
+    ones_ref[...] = (row // phases == column_id // phases).astype(F32).astype(BF16)
     loads[4].wait()
     strips_ref[...] = exact_dot(left + right, strip_ref[:width])
     loads[5].wait()
@@ -197,7 +204,7 @@
 
 
 def relax(
-    got, fine, pin, rate_ref, strips_ref, main_ref, strip_ref, label_ref, *rest
+    got, fine, pin, rate_ref, strips_ref, beside_ref, ones_ref, main_ref, strip_ref, label_ref, *rest
 ):
     out_hbm, p1, out_ref, out_sem = rest
     fy, phases, width = fine.shape
@@ -266,42 +273,65 @@
         row = got[5, n : n + 1] if y < 0 else got[2, n : n + 1]
         return jnp.where(jnp.broadcast_to(row, shape) == phase_f, rate, 0.0)
 
-    def first_step(y, prev, cur, nxt):
-        if y < 0:
-            beside_row = corner
-        elif y == fy:
-            beside_row = turn(corner, 2)
-        else:
-            beside_row = turn(side, -2 * y)
+    def halves(v):
+        high = v.astype(BF16)
+        return high, (v - high.astype(F32)).astype(BF16)
+
+    def mixed(rows):
+        flat = rows.reshape(-1, width)
+        near = jnp.dot(
+            jnp.concatenate(halves(flat), axis=1), beside_ref[...], preferred_element_type=F32
+        )
+        squares = jnp.dot(
+            ones_ref[...], jnp.concatenate(halves(flat * flat), axis=0), preferred_element_type=F32
+        )
+        return near.reshape(rows.shape), squares.reshape(rows.shape)
+
+    def sides(strip, block):
+        at = range(8 * block, 8 * block + 8)
+        return jnp.stack([jnp.where(ends, turn(strip, -2 * y), 0.0) for y in at])
+
+    def first_row(y, prev, cur, nxt, beside_row):
         base = cur + rate * (prev + nxt + around(cur, beside_row) - cur * (4.0 + total(cur)))
         for n in range(2):
             p1[n, y + 1] = base + pinned(n, y)
 
+    def first_step(block):
+        rows = [fine_row(y) for y in range(8 * block - 1, 8 * block + 9)]
+        cur = jnp.stack(rows[1:9])
+        near, squares = mixed(cur)
+        near = near + sides(side, block) + jnp.stack(rows[:8]) + jnp.stack(rows[2:])
+        base = cur + rate * (near - cur * (4.0 + squares))
+        for n in range(2):
+            p1[n, 8 * block + 1 : 8 * block + 9] = base + pin[n, 8 * block : 8 * block + 8]
+
+    out_rows = out_ref.reshape(fy // 8 * phases * 16, width)
+
     def second_step(block):
-        done = [[], []]
-        for y in range(8 * block, 8 * block + 8):
-            both = [p1[n, y + 1] for n in range(2)]
-            for n in range(2):
-                c = both[n]
-                near = p1[n, y] + p1[n, y + 2] + around(c, turn(side1[n], -2 * y))
-                near = near + 2.0 * both[1 - n]
-                done[n].append(c + rate * (near - c * (6.0 + total(c))) + pinned(n, y))
+        y = 8 * block
+        both = [p1[n, y + 1 : y + 9] for n in range(2)]
         for n in range(2):
-            out_ref[block, :, n] = jnp.swapaxes(jnp.stack(done[n]), 0, 1)
+            cur = both[n]
+            near, squares = mixed(cur)
+            near = near + sides(side1[n], block) + p1[n, y : y + 8] + p1[n, y + 2 : y + 10]
+            near = near + 2.0 * both[1 - n]
+            new = cur + rate * (near - cur * (6.0 + squares)) + pin[n, y : y + 8]
+            for j in range(8):
+                out_rows[pl.ds(block * phases * 16 + 8 * n + j, phases, stride=16)] = new[j]
         copy = pltpu.make_async_copy(
-            out_ref.at[block], out_hbm.at[:, :, pl.ds(8 * block, 8)], out_sem.at[block]
+            out_ref.at[block], out_hbm.at[:, :, pl.ds(y, 8)], out_sem.at[block]
         )
         copy.start()
         return copy
 
     copies = []
-    prev, cur = fine_row(-2), fine_row(-1)
-    for y in range(-1, fy + 1):
-        nxt = fine_row(y + 1)
-        first_step(y, prev, cur, nxt)
-        prev, cur = cur, nxt
-        if y > 0 and y % 8 == 0:
-            copies.append(second_step(y // 8 - 1))
+    first_row(-1, fine_row(-2), fine_row(-1), fine_row(0), corner)
+    first_row(fy, fine_row(fy - 1), fine_row(fy), fine_row(fy + 1), turn(corner, 2))
+    first_step(0)
+    for block in range(1, fy // 8):
+        first_step(block)
+        copies.append(second_step(block - 1))
+    copies.append(second_step(fy // 8 - 1))
     for copy in copies:
         copy.wait()
 
@@ -323,6 +353,8 @@
         pltpu.VMEM((2, 2 * ny, phases, width), F32),
         pltpu.VMEM((phases, width), F32),
         pltpu.VMEM((phases, 4 * width), F32),
+        pltpu.VMEM((2 * width, width), BF16),
+        pltpu.VMEM((8 * phases, 16 * phases), BF16),
         *(pltpu.VMEM(v.shape, v.dtype) for v in weights),
     ]
     parts = pl.pallas_call(

time: 12 us -> 11.8 us (0.983)
  Pallas kernels: 11.9 us -> 11.6 us
    pallas_call x1, Pallas kernels: 2.28 us -> 2.01 us  [shards(): pl.pallas_call(relax, out_shape=jax.ShapeDtypeStruct((phases, 2, 2 * ny,...]
where the time goes in v5:
time: 11.8 us; the launch traced here: 11.6 us
  Pallas kernels  11.6 us (98%)
    pallas_call x1, Pallas kernels, shards(): pl.pallas_call(functools.partial(exchange, gy, gz), out_shape=shared, in_...  9.6 us
    pallas_call x1, Pallas kernels, shards(): pl.pallas_call(relax, out_shape=jax.ShapeDtypeStruct((phases, 2, 2 * ny,...  2.01 us

profile of v5, /device:TPU:0, one launch (start us, length us, event | category | flops | bytes accessed | tf_op | source)
XLA Modules:
  0.0 11.6 jit_solution(5416790876736196185)
XLA Ops:
  0.0 9.6 %exchange.1 = (f32[20,8,128]{2,1,0:T(8,128)S(1)}, f32[64,8,128]{2,1,0:T(8,128)S(1)}, f32[2,64,8,128]{3,2,1,0:T(8,128)S(1)}, f32[8,128]{1,0:T(8,128)S(1)}, f32[8,...) custom-call(f32[8,1,32,64]{3,2,1,0:T(8,128)} %refs_0_.1, ...), custom_call_target="tpu_custom_call" | custom-call | tf_op jit(solution)/shard_map/exchange/pallas_call | solution.py:360
  9.6 2.0 %relax.1 = f32[8,2,64,128]{3,2,1,0:T(8,128)} custom-call(f32[20,8,128]{2,1,0:T(8,128)S(1)} %get-tuple-element.15.got, f32[64,8,128]{2,1,0:T(8,128)S(1)} %get-tuple-element.16.fine, f32[2,64,8,128]{3,2,1,0:T(8,128)S(1)} %get-tuple-element.17.pin, f32[8,128]{1,0:T(8,128)S(1)} %get-tuple-element.18.rate_ref, f32[8,512]{1,0:T(8,128)S(1)} %get-tuple-element.19.strips_ref, ...), custom_call_target="tpu_custom_call" | custom-call | tf_op jit(solution)/shard_map/relax/pallas_call | solution.py:379

commit v6 on v5

--- a/solution.py
+++ b/solution.py
@@ -80,14 +80,14 @@
 
 
 PARTS = (
-    ((-1, 0), (0, 3), (0, 3)),
-    ((1, 0), (3, 6), (3, 6)),
-    ((0, -1), (6, 8), (6, 8)),
-    ((0, 1), (8, 10), (8, 10)),
     ((-1, -1), (0, 2), (10, 12)),
     ((-1, 1), (0, 2), (12, 14)),
     ((1, -1), (3, 5), (14, 16)),
     ((1, 1), (3, 5), (16, 18)),
+    ((0, -1), (6, 8), (6, 8)),
+    ((0, 1), (8, 10), (8, 10)),
+    ((-1, 0), (0, 3), (0, 3)),
+    ((1, 0), (3, 6), (3, 6)),
 )
 SLOTS = 20
 
@@ -282,13 +282,19 @@
         near = jnp.dot(
             jnp.concatenate(halves(flat), axis=1), beside_ref[...], preferred_element_type=F32
         )
-        squares = jnp.dot(
-            ones_ref[...], jnp.concatenate(halves(flat * flat), axis=0), preferred_element_type=F32
-        )
+        tall = 8 * phases
+        squares = [
+            jnp.dot(
+                ones_ref[...],
+                jnp.concatenate(halves(part * part), axis=0),
+                preferred_element_type=F32,
+            )
+            for part in (flat[at : at + tall] for at in range(0, flat.shape[0], tall))
+        ]
+        squares = jnp.concatenate(squares, axis=0)
         return near.reshape(rows.shape), squares.reshape(rows.shape)
 
-    def sides(strip, block):
-        at = range(8 * block, 8 * block + 8)
+    def sides(strip, at):
         return jnp.stack([jnp.where(ends, turn(strip, -2 * y), 0.0) for y in at])
 
     def first_row(y, prev, cur, nxt, beside_row):
@@ -296,42 +302,41 @@
         for n in range(2):
             p1[n, y + 1] = base + pinned(n, y)
 
-    def first_step(block):
-        rows = [fine_row(y) for y in range(8 * block - 1, 8 * block + 9)]
-        cur = jnp.stack(rows[1:9])
+    def first_step():
+        rows = [fine_row(y) for y in range(-1, fy + 1)]
+        cur = jnp.stack(rows[1:-1])
         near, squares = mixed(cur)
-        near = near + sides(side, block) + jnp.stack(rows[:8]) + jnp.stack(rows[2:])
+        near = near + sides(side, range(fy)) + jnp.stack(rows[:-2]) + jnp.stack(rows[2:])
         base = cur + rate * (near - cur * (4.0 + squares))
         for n in range(2):
-            p1[n, 8 * block + 1 : 8 * block + 9] = base + pin[n, 8 * block : 8 * block + 8]
-
-    out_rows = out_ref.reshape(fy // 8 * phases * 16, width)
-
-    def second_step(block):
-        y = 8 * block
-        both = [p1[n, y + 1 : y + 9] for n in range(2)]
+            p1[n, 1 : fy + 1] = base + pin[n]
+
+    chunks, _, _, tall, _ = out_ref.shape
+    out_rows = out_ref.reshape(chunks * phases * 2 * tall, width)
+
+    def second_step(chunk):
+        y = tall * chunk
+        both = [p1[n, y + 1 : y + tall + 1] for n in range(2)]
         for n in range(2):
             cur = both[n]
             near, squares = mixed(cur)
-            near = near + sides(side1[n], block) + p1[n, y : y + 8] + p1[n, y + 2 : y + 10]
+            near = near + sides(side1[n], range(y, y + tall))
+            near = near + p1[n, y : y + tall] + p1[n, y + 2 : y + tall + 2]
             near = near + 2.0 * both[1 - n]
-            new = cur + rate * (near - cur * (6.0 + squares)) + pin[n, y : y + 8]
-            for j in range(8):
-                out_rows[pl.ds(block * phases * 16 + 8 * n + j, phases, stride=16)] = new[j]
+            new = cur + rate * (near - cur * (6.0 + squares)) + pin[n, y : y + tall]
+            for j in range(tall):
+                at = (chunk * phases * 2 + n) * tall + j
+                out_rows[pl.ds(at, phases, stride=2 * tall)] = new[j]
         copy = pltpu.make_async_copy(
-            out_ref.at[block], out_hbm.at[:, :, pl.ds(y, 8)], out_sem.at[block]
+            out_ref.at[chunk], out_hbm.at[:, :, pl.ds(y, tall)], out_sem.at[chunk]
         )
         copy.start()
         return copy
 
-    copies = []
     first_row(-1, fine_row(-2), fine_row(-1), fine_row(0), corner)
     first_row(fy, fine_row(fy - 1), fine_row(fy), fine_row(fy + 1), turn(corner, 2))
-    first_step(0)
-    for block in range(1, fy // 8):
-        first_step(block)
-        copies.append(second_step(block - 1))
-    copies.append(second_step(fy // 8 - 1))
+    first_step()
+    copies = [second_step(chunk) for chunk in range(chunks)]
     for copy in copies:
         copy.wait()
 
@@ -383,8 +388,8 @@
         out_specs=hbm,
         scratch_shapes=[
             pltpu.VMEM((2, 2 * ny + 2, phases, width), F32),
-            pltpu.VMEM((2 * ny // 8, phases, 2, 8, width), F32),
-            pltpu.SemaphoreType.DMA((2 * ny // 8,)),
+            pltpu.VMEM((2, phases, 2, ny, width), F32),
+            pltpu.SemaphoreType.DMA((2,)),
         ],
         compiler_params=pltpu.CompilerParams(vmem_limit_bytes=8 * 2**20),
         name="relax",

time: 11.8 us -> 11.6 us (0.983)
  Pallas kernels: 11.6 us -> 11.4 us
    pallas_call x1, Pallas kernels: 2.01 us -> 1.89 us  [shards(): pl.pallas_call(relax, out_shape=jax.ShapeDtypeStruct((phases, 2, 2 * ny,...]
where the time goes in v6:
time: 11.6 us; the launch traced here: 11.4 us
  Pallas kernels  11.4 us (98%)
    pallas_call x1, Pallas kernels, shards(): pl.pallas_call(functools.partial(exchange, gy, gz), out_shape=shared, in_...  9.52 us
    pallas_call x1, Pallas kernels, shards(): pl.pallas_call(relax, out_shape=jax.ShapeDtypeStruct((phases, 2, 2 * ny,...  1.89 us

profile of v6, /device:TPU:0, one launch (start us, length us, event | category | flops | bytes accessed | tf_op | source)
XLA Modules:
  0.0 11.4 jit_solution(8288487945527352622)
XLA Ops:
  0.0 9.5 %exchange.1 = (f32[20,8,128]{2,1,0:T(8,128)S(1)}, f32[64,8,128]{2,1,0:T(8,128)S(1)}, f32[2,64,8,128]{3,2,1,0:T(8,128)S(1)}, f32[8,128]{1,0:T(8,128)S(1)}, f32[8,...) custom-call(f32[8,1,32,64]{3,2,1,0:T(8,128)} %refs_0_.1, ...), custom_call_target="tpu_custom_call" | custom-call | tf_op jit(solution)/shard_map/exchange/pallas_call | solution.py:365
  9.5 1.9 %relax.1 = f32[8,2,64,128]{3,2,1,0:T(8,128)} custom-call(f32[20,8,128]{2,1,0:T(8,128)S(1)} %get-tuple-element.15.got, f32[64,8,128]{2,1,0:T(8,128)S(1)} %get-tuple-element.16.fine, f32[2,64,8,128]{3,2,1,0:T(8,128)S(1)} %get-tuple-element.17.pin, f32[8,128]{1,0:T(8,128)S(1)} %get-tuple-element.18.rate_ref, f32[8,512]{1,0:T(8,128)S(1)} %get-tuple-element.19.strips_ref, ...), custom_call_target="tpu_custom_call" | custom-call | tf_op jit(solution)/shard_map/relax/pallas_call | solution.py:384

commit v7 on v4

--- a/solution.py
+++ b/solution.py
@@ -37,20 +37,22 @@
 
     def where(r, c):
         if r == -1:
-            return 2 * width + col_lane(c, nz)
+            return 3 * width + col_lane(c, nz)
         if r == ny:
-            return 2 * width + (col_lane(c, nz) + 8) % width
+            return 3 * width + (col_lane(c, nz) + 8) % width
         assert 0 <= r < ny
         if c in (0, 1):
             return 2 * r + c
         if c in (nz - 2, nz - 1):
             return 2 * ny + 2 * r + c - (nz - 2)
+        if c in (2, nz - 3):
+            return width + (2 * r + c) % width
         if c in (nz, nz + 1):
-            return width + 2 * r + c - nz
+            return 2 * width + 2 * r + c - nz
         assert c in (-2, -1)
-        return width + 2 * ny + 2 * r + c + 2
-
-    w = np.zeros((3 * width, 4 * width), np.float32)
+        return 2 * width + 2 * ny + 2 * r + c + 2
+
+    w = np.zeros((4 * width, 8 * width), np.float32)
 
     def put(y, z, out):
         for r, a in taps(y):
@@ -59,9 +61,9 @@
 
     for y in range(2 * ny):
         left, right = 2 * y, (2 * y - 1) % width
-        for block, (zl, zr) in enumerate(((-2, width + 1), (-1, width), (0, width - 1))):
-            put(y, zl, block * width + left)
-            put(y, zr, block * width + right)
+        for block, k in ((0, -2), (1, -1), (2, 0), (4, 1), (5, 2), (6, 3), (7, 4)):
+            put(y, k, block * width + left)
+            put(y, width - 1 - k, block * width + right)
     put(-1, -1, 3 * width)
     put(-1, width, 3 * width + width - 1)
     put(2 * ny, -1, 3 * width + width - 2)
@@ -80,14 +82,14 @@
 
 
 PARTS = (
-    ((-1, 0), (0, 3), (0, 3)),
-    ((1, 0), (3, 6), (3, 6)),
-    ((0, -1), (6, 8), (6, 8)),
-    ((0, 1), (8, 10), (8, 10)),
     ((-1, -1), (0, 2), (10, 12)),
     ((-1, 1), (0, 2), (12, 14)),
     ((1, -1), (3, 5), (14, 16)),
     ((1, 1), (3, 5), (16, 18)),
+    ((0, -1), (6, 8), (6, 8)),
+    ((0, 1), (8, 10), (8, 10)),
+    ((-1, 0), (0, 3), (0, 3)),
+    ((1, 0), (3, 6), (3, 6)),
 )
 SLOTS = 20
 
@@ -103,10 +105,34 @@
     return product[: x.shape[0]] + product[x.shape[0] :]
 
 
+def halves(v):
+    high = v.astype(BF16)
+    return high, (v - high.astype(F32)).astype(BF16)
+
+
+def mixed(rows, beside, ones):
+    _, phases, width = rows.shape
+    flat = rows.reshape(-1, width)
+    near = jnp.dot(jnp.concatenate(halves(flat), axis=1), beside, preferred_element_type=F32)
+    tall = 8 * phases
+    squares = [
+        jnp.dot(
+            ones, jnp.concatenate(halves(part * part), axis=0), preferred_element_type=F32
+        )
+        for part in (flat[at : at + tall] for at in range(0, flat.shape[0], tall))
+    ]
+    return near.reshape(rows.shape), jnp.concatenate(squares, axis=0).reshape(rows.shape)
+
+
+def above_below(rows):
+    return jnp.concatenate([rows[:1], rows[:-1]]) + jnp.concatenate([rows[1:], rows[-1:]])
+
+
 def exchange(gy, gz, *refs):
     sources, refs = refs[:6], refs[6:]
-    got, fine_ref, pin_ref, rate_ref, strips_ref, main_ref, strip_ref, label_ref = refs[:8]
-    mobility_ref, labels_ref, coarse_ref, stage, send_sem, recv_sem, load_sem = refs[8:]
+    got, fine_ref, inner_ref, pin_ref, rate_ref, strips_ref, side_pin_ref = refs[:7]
+    main_ref, strip_ref, label_ref = refs[7:10]
+    mobility_ref, labels_ref, coarse_ref, stage, send_sem, recv_sem, load_sem = refs[10:]
     me_y, me_z = lax.axis_index("gy"), lax.axis_index("gz")
 
     def other(dy, dz):
@@ -182,6 +208,7 @@
     rate_ref[...] = rate
     loads[3].wait()
     fine_z = exact_dot(x.reshape(-1, width), main_ref[...]).reshape(ny, phases, width)
+    fine_ref[0], fine_ref[2 * ny - 1] = fine_z[0], fine_z[ny - 1]
     for y in range(1, 2 * ny - 1):
         (r0, a), (r1, b) = taps(y)
         fine_ref[y] = a * fine_z[r0] + b * fine_z[r1]
@@ -189,23 +216,54 @@
         for y in range(2 * ny):
             label = jnp.broadcast_to(labels_ref[n, y : y + 1], rate.shape)
             pin_ref[n, y] = jnp.where(label == phase_id, rate, 0.0)
+
     loads[4].wait()
-    strips_ref[...] = exact_dot(left + right, strip_ref[:width])
+    third = jnp.zeros((phases, width), F32)
+    for r in range(ny):
+        hit = (lane == (2 * r + 2) % width) | (lane == (2 * r + nz - 3) % width)
+        third = jnp.where(hit, pltpu.roll(rows[r], 2 * r, 1) if r else rows[r], third)
+    strips_ref[...] = exact_dot(
+        jnp.concatenate([left + right, third], axis=1), strip_ref[: 2 * width]
+    )
     loads[5].wait()
+    edge_lane = jnp.where(phase_id < 4, phase_id, width - 1 - (phase_id - 4))
+    edge_labels = lax.dot_general(
+        (lane == edge_lane).astype(BF16), flat, (((1,), (1,)), ((), ())), preferred_element_type=F32
+    ).astype(BF16)
+    from_left = jnp.dot(edge_labels, label_ref[:width], preferred_element_type=F32)
+    from_right = jnp.dot(edge_labels, label_ref[width:], preferred_element_type=F32)
+    for k in range(4):
+        label = from_left[k : k + 1] + from_right[4 + k : 5 + k]
+        for n in range(2):
+            one = jnp.broadcast_to(label[:, n * width : (n + 1) * width], rate.shape)
+            side_pin_ref[k, n] = jnp.where(one == phase_id.astype(F32), rate, 0.0)
+
+    row = lax.broadcasted_iota(jnp.int32, (2 * width, width), 0) % width
+    column_id = lax.broadcasted_iota(jnp.int32, (2 * width, width), 1)
+    beside = (jnp.abs(row - column_id) == 1).astype(F32).astype(BF16)
+    row = lax.broadcasted_iota(jnp.int32, (8 * phases, 16 * phases), 0)
+    column_id = lax.broadcasted_iota(jnp.int32, (8 * phases, 16 * phases), 1) % (8 * phases)
+    ones = (row // phases == column_id // phases).astype(F32).astype(BF16)
+    cur = fine_ref[...]
+    near, squares = mixed(cur, beside, ones)
+    base = cur + rate * (near + above_below(cur) - cur * (4.0 + squares))
+    both = [base + pin_ref[n] for n in range(2)]
+    for n in range(2):
+        cur = both[n]
+        near, squares = mixed(cur, beside, ones)
+        near = near + above_below(cur) + 2.0 * both[1 - n]
+        inner_ref[n] = cur + rate * (near - cur * (6.0 + squares)) + pin_ref[n]
     for copy in copies:
         copy.wait()
 
 
-def relax(
-    got, fine, pin, rate_ref, strips_ref, main_ref, strip_ref, label_ref, *rest
-):
-    out_hbm, p1, out_ref, out_sem = rest
+def relax(got, fine, inner, pin, rate_ref, strips_ref, side_pin, main_ref, strip_ref, label_ref, *rest):
+    out_hbm, out_ref, out_sem = rest
     fy, phases, width = fine.shape
     ny, nz = fy // 2, width // 2
     shape = (phases, width)
     lane = lax.broadcasted_iota(jnp.int32, shape, 1)
-    phase_id = lax.broadcasted_iota(jnp.int32, shape, 0)
-    phase_f = phase_id.astype(F32)
+    phase_f = lax.broadcasted_iota(jnp.int32, shape, 0).astype(F32)
     rate = rate_ref[...]
     first, last = lane == 0, lane == width - 1
     ends = first | last
@@ -239,18 +297,41 @@
     beside = jnp.where(lane < 2 * ny, got[6], got[8])
     near = (lane < 4) | (lane >= nz - 4) & (lane < nz + 4) | (lane >= width - 4)
     rim = jnp.where(near, above[1], turn(below[0], 8))
-    strips = exact_dot(jnp.concatenate([beside, rim], axis=1), strip_ref[width:])
+    strips = exact_dot(jnp.concatenate([beside, rim], axis=1), strip_ref[2 * width :])
     strips = strips + strips_ref[...]
-    outer, side, inner, corner = (strips[:, n * width : (n + 1) * width] for n in range(4))
+    blocks = [strips[:, n * width : (n + 1) * width] for n in range(8)]
+    corner = blocks.pop(3)
+    fine_at = dict(zip(range(-2, 5), blocks))
     near_labels = jnp.concatenate([got[9], got[7]], axis=1).astype(BF16)
     strip_labels = jnp.dot(near_labels, label_ref[...], preferred_element_type=F32)
-    up = jnp.where(ends, corner, turn(side, 2))
-    down = jnp.where((lane == width - 2) | (lane == width - 3), corner, turn(side, -2))
-    side_base = side + rate * (outer + inner + up + down - side * (4.0 + total(side)))
-    side1 = [
-        side_base + jnp.where(strip_labels[:, n * width : (n + 1) * width] == phase_f, rate, 0.0)
-        for n in range(2)
-    ]
+
+    def side_pinned(k, n):
+        if k >= 0:
+            return side_pin[k, n]
+        return jnp.where(strip_labels[:, n * width : (n + 1) * width] == phase_f, rate, 0.0)
+
+    step1 = {}
+    for k in range(-1, 4):
+        c = fine_at[k]
+        up, down = turn(c, 2), turn(c, -2)
+        if k < 0:
+            up = jnp.where(ends, corner, up)
+            down = jnp.where((lane == width - 2) | (lane == width - 3), corner, down)
+        near = fine_at[k - 1] + fine_at[k + 1] + up + down
+        base = c + rate * (near - c * (4.0 + total(c)))
+        step1[k] = [base + side_pinned(k, n) for n in range(2)]
+    side, side1 = fine_at[-1], step1[-1]
+    step2 = {}
+    for k in range(3):
+        step2[k] = []
+        for n in range(2):
+            c = step1[k][n]
+            near = step1[k - 1][n] + step1[k + 1][n] + turn(c, 2) + turn(c, -2)
+            near = near + 2.0 * step1[k][1 - n]
+            new = c + rate * (near - c * (6.0 + total(c))) + side_pin[k, n]
+            if k:
+                new = jnp.where(lane % 2 == k % 2, turn(new, k), turn(new, -k))
+            step2[k].append(new)
 
     def fine_row(y):
         if 0 < y < fy - 1:
@@ -258,7 +339,7 @@
         else:
             (r0, a), (r1, b) = taps(y)
             v = a * at_rim[r0] + b * at_rim[r1]
-        return jnp.where(ends, turn(inner, -2 * y), v) if 0 <= y < fy else v
+        return jnp.where(ends, turn(fine_at[0], -2 * y), v) if 0 <= y < fy else v
 
     def pinned(n, y):
         if 0 <= y < fy:
@@ -266,7 +347,8 @@
         row = got[5, n : n + 1] if y < 0 else got[2, n : n + 1]
         return jnp.where(jnp.broadcast_to(row, shape) == phase_f, rate, 0.0)
 
-    def first_step(y, prev, cur, nxt):
+    def first_row(y):
+        prev, cur, nxt = (fine_row(v) for v in (y - 1, y, y + 1))
         if y < 0:
             beside_row = corner
         elif y == fy:
@@ -274,34 +356,36 @@
         else:
             beside_row = turn(side, -2 * y)
         base = cur + rate * (prev + nxt + around(cur, beside_row) - cur * (4.0 + total(cur)))
+        return [base + pinned(n, y) for n in range(2)]
+
+    rim1 = {y: first_row(y) for y in (*range(-1, 4), *range(fy - 4, fy + 1))}
+    at_column = [(lane == k) | (lane == width - 1 - k) for k in range(3)]
+
+    def second_row(n, y):
+        if 3 <= y < fy - 3:
+            new = inner[n, y]
+            for k in range(3):
+                new = jnp.where(at_column[k], turn(step2[k][n], -2 * y), new)
+            return new
+        c = rim1[y][n]
+        near = rim1[y - 1][n] + rim1[y + 1][n] + around(c, turn(side1[n], -2 * y))
+        near = near + 2.0 * rim1[y][1 - n]
+        return c + rate * (near - c * (6.0 + total(c))) + pinned(n, y)
+
+    chunks, _, _, tall, _ = out_ref.shape
+    out_rows = out_ref.reshape(chunks * phases * 2 * tall, width)
+    copies = []
+    for chunk in range(chunks):
         for n in range(2):
-            p1[n, y + 1] = base + pinned(n, y)
-
-    def second_step(block):
-        done = [[], []]
-        for y in range(8 * block, 8 * block + 8):
-            both = [p1[n, y + 1] for n in range(2)]
-            for n in range(2):
-                c = both[n]
-                near = p1[n, y] + p1[n, y + 2] + around(c, turn(side1[n], -2 * y))
-                near = near + 2.0 * both[1 - n]
-                done[n].append(c + rate * (near - c * (6.0 + total(c))) + pinned(n, y))
-        for n in range(2):
-            out_ref[block, :, n] = jnp.swapaxes(jnp.stack(done[n]), 0, 1)
+            for j in range(tall):
+                at = (chunk * phases * 2 + n) * tall + j
+                row = second_row(n, chunk * tall + j)
+                out_rows[pl.ds(at, phases, stride=2 * tall)] = row
         copy = pltpu.make_async_copy(
-            out_ref.at[block], out_hbm.at[:, :, pl.ds(8 * block, 8)], out_sem.at[block]
+            out_ref.at[chunk], out_hbm.at[:, :, pl.ds(chunk * tall, tall)], out_sem.at[chunk]
         )
         copy.start()
-        return copy
-
-    copies = []
-    prev, cur = fine_row(-2), fine_row(-1)
-    for y in range(-1, fy + 1):
-        nxt = fine_row(y + 1)
-        first_step(y, prev, cur, nxt)
-        prev, cur = cur, nxt
-        if y > 0 and y % 8 == 0:
-            copies.append(second_step(y // 8 - 1))
+        copies.append(copy)
     for copy in copies:
         copy.wait()
 
@@ -321,8 +405,10 @@
         pltpu.VMEM((SLOTS, phases, width), F32),
         pltpu.VMEM((2 * ny, phases, width), F32),
         pltpu.VMEM((2, 2 * ny, phases, width), F32),
+        pltpu.VMEM((2, 2 * ny, phases, width), F32),
         pltpu.VMEM((phases, width), F32),
-        pltpu.VMEM((phases, 4 * width), F32),
+        pltpu.VMEM((phases, 8 * width), F32),
+        pltpu.VMEM((4, 2, phases, width), F32),
         *(pltpu.VMEM(v.shape, v.dtype) for v in weights),
     ]
     parts = pl.pallas_call(
@@ -340,7 +426,7 @@
             pltpu.SemaphoreType.DMA((len(sources),)),
         ],
         compiler_params=pltpu.CompilerParams(
-            collective_id=0, has_side_effects=True, vmem_limit_bytes=8 * 2**20
+            collective_id=0, has_side_effects=True, vmem_limit_bytes=12 * 2**20
         ),
         name="exchange",
     )(*sources)
@@ -350,11 +436,10 @@
         in_specs=[vmem] * len(shared),
         out_specs=hbm,
         scratch_shapes=[
-            pltpu.VMEM((2, 2 * ny + 2, phases, width), F32),
-            pltpu.VMEM((2 * ny // 8, phases, 2, 8, width), F32),
-            pltpu.SemaphoreType.DMA((2 * ny // 8,)),
+            pltpu.VMEM((2, phases, 2, ny, width), F32),
+            pltpu.SemaphoreType.DMA((2,)),
         ],
-        compiler_params=pltpu.CompilerParams(vmem_limit_bytes=8 * 2**20),
+        compiler_params=pltpu.CompilerParams(vmem_limit_bytes=12 * 2**20),
         name="relax",
     )(*parts)
 

time: 12 us -> 11.5 us (0.958)
  Pallas kernels: 11.9 us -> 11.4 us
    pallas_call x1, Pallas kernels: 2.28 us -> 1.86 us  [shards(): pl.pallas_call(relax, out_shape=jax.ShapeDtypeStruct((phases, 2, 2 * ny,...]
where the time goes in v7:
time: 11.5 us; the launch traced here: 11.4 us
  Pallas kernels  11.4 us (99%)
    pallas_call x1, Pallas kernels, shards(): pl.pallas_call(functools.partial(exchange, gy, gz), out_shape=shared, in_...  9.52 us
    pallas_call x1, Pallas kernels, shards(): pl.pallas_call(relax, out_shape=jax.ShapeDtypeStruct((phases, 2, 2 * ny,...  1.86 us

profile of v7, /device:TPU:0, one launch (start us, length us, event | category | flops | bytes accessed | tf_op | source)
XLA Modules:
  0.0 11.4 jit_solution(576734430960259924)
XLA Ops:
  0.0 9.5 %exchange.1 = (f32[20,8,128]{2,1,0:T(8,128)S(1)}, f32[64,8,128]{2,1,0:T(8,128)S(1)}, f32[2,64,8,128]{3,2,1,0:T(8,128)S(1)}, f32[2,64,8,128]{3,2,1,0:T(8,128)S(1)...) custom-call(f32[8,1,32,64]{3,2,1,0:T(8,128)} %refs_0_.1, ...), custom_call_target="tpu_custom_call" | custom-call | tf_op jit(solution)/shard_map/exchange/pallas_call | solution.py:414
  9.5 1.9 %relax.1 = f32[8,2,64,128]{3,2,1,0:T(8,128)} custom-call(f32[20,8,128]{2,1,0:T(8,128)S(1)} %get-tuple-element.15.got, f32[64,8,128]{2,1,0:T(8,128)S(1)} %get-tuple-element.16.fine, f32[2,64,8,128]{3,2,1,0:T(8,128)S(1)} %get-tuple-element.17.inner, f32[2,64,8,128]{3,2,1,0:T(8,128)S(1)} %get-tuple-element.18.pin, f32[8,128]{1,0:T(8,128)S(1)} %get-tuple-element.19.rate_ref, ...), custom_call_target="tpu_custom_call" | custom-call | tf_op jit(solution)/shard_map/relax/pallas_call | solution.py:433

commit v8 on v7

--- a/solution.py
+++ b/solution.py
@@ -299,9 +299,9 @@
     rim = jnp.where(near, above[1], turn(below[0], 8))
     strips = exact_dot(jnp.concatenate([beside, rim], axis=1), strip_ref[2 * width :])
     strips = strips + strips_ref[...]
-    blocks = [strips[:, n * width : (n + 1) * width] for n in range(8)]
-    corner = blocks.pop(3)
-    fine_at = dict(zip(range(-2, 5), blocks))
+    pieces = [strips[:, n * width : (n + 1) * width] for n in range(8)]
+    corner = pieces.pop(3)
+    fine_at = dict(zip(range(-2, 5), pieces))
     near_labels = jnp.concatenate([got[9], got[7]], axis=1).astype(BF16)
     strip_labels = jnp.dot(near_labels, label_ref[...], preferred_element_type=F32)
 
@@ -361,33 +361,49 @@
     rim1 = {y: first_row(y) for y in (*range(-1, 4), *range(fy - 4, fy + 1))}
     at_column = [(lane == k) | (lane == width - 1 - k) for k in range(3)]
 
+    def merged(row, columns, by):
+        for k in range(3):
+            row = jnp.where(at_column[k], turn(columns[k], by), row)
+        return row
+
     def second_row(n, y):
         if 3 <= y < fy - 3:
-            new = inner[n, y]
-            for k in range(3):
-                new = jnp.where(at_column[k], turn(step2[k][n], -2 * y), new)
-            return new
+            return merged(inner[n, y], [step2[k][n] for k in range(3)], -2 * y)
         c = rim1[y][n]
         near = rim1[y - 1][n] + rim1[y + 1][n] + around(c, turn(side1[n], -2 * y))
         near = near + 2.0 * rim1[y][1 - n]
         return c + rate * (near - c * (6.0 + total(c))) + pinned(n, y)
 
-    chunks, _, _, tall, _ = out_ref.shape
-    out_rows = out_ref.reshape(chunks * phases * 2 * tall, width)
-    copies = []
-    for chunk in range(chunks):
+    blocks, _, _, tall, _ = out_ref.shape
+    out_rows = out_ref.reshape(blocks, phases * 2 * tall, width)
+
+    def send(block):
+        return pltpu.make_async_copy(
+            out_ref.at[block],
+            out_hbm.at[:, :, pl.ds(pl.multiple_of(block * tall, tall), tall)],
+            out_sem.at[block],
+        )
+
+    def store(block, n, j, row):
+        out_rows[block, pl.ds(n * tall + j, phases, stride=2 * tall)] = row
+
+    for block in (0, blocks - 1):
         for n in range(2):
             for j in range(tall):
-                at = (chunk * phases * 2 + n) * tall + j
-                row = second_row(n, chunk * tall + j)
-                out_rows[pl.ds(at, phases, stride=2 * tall)] = row
-        copy = pltpu.make_async_copy(
-            out_ref.at[chunk], out_hbm.at[:, :, pl.ds(chunk * tall, tall)], out_sem.at[chunk]
-        )
-        copy.start()
-        copies.append(copy)
-    for copy in copies:
-        copy.wait()
+                store(block, n, j, second_row(n, block * tall + j))
+        send(block).start()
+
+    def body(block, columns):
+        columns = [[turn(v, -2 * tall) for v in plane] for plane in columns]
+        for n in range(2):
+            for j in range(tall):
+                store(block, n, j, merged(inner[n, block * tall + j], columns[n], -2 * j))
+        send(block).start()
+        return columns
+
+    lax.fori_loop(1, blocks - 1, body, [[step2[k][n] for k in range(3)] for n in range(2)])
+    for block in range(blocks):
+        send(block).wait()
 
 
 def shards(gy, gz, coarse, labels, mobility):
@@ -436,8 +452,8 @@
         in_specs=[vmem] * len(shared),
         out_specs=hbm,
         scratch_shapes=[
-            pltpu.VMEM((2, phases, 2, ny, width), F32),
-            pltpu.SemaphoreType.DMA((2,)),
+            pltpu.VMEM((2 * ny // 8, phases, 2, 8, width), F32),
+            pltpu.SemaphoreType.DMA((2 * ny // 8,)),
         ],
         compiler_params=pltpu.CompilerParams(vmem_limit_bytes=12 * 2**20),
         name="relax",

time: 11.5 us -> 12.1 us (1.052)
  Pallas kernels: 11.4 us -> 12 us
    pallas_call x1, Pallas kernels: 1.86 us -> 2.46 us  [shards(): pl.pallas_call(relax, out_shape=jax.ShapeDtypeStruct((phases, 2, 2 * ny,...]
where the time goes in v8:
time: 12.1 us; the launch traced here: 12 us
  Pallas kernels  12 us (99%)
    pallas_call x1, Pallas kernels, shards(): pl.pallas_call(functools.partial(exchange, gy, gz), out_shape=shared, in_...  9.52 us
    pallas_call x1, Pallas kernels, shards(): pl.pallas_call(relax, out_shape=jax.ShapeDtypeStruct((phases, 2, 2 * ny,...  2.46 us

profile of v8, /device:TPU:0, one launch (start us, length us, event | category | flops | bytes accessed | tf_op | source)
XLA Modules:
  0.0 12.0 jit_solution(3413278553727343277)
XLA Ops:
  0.0 9.5 %exchange.1 = (f32[20,8,128]{2,1,0:T(8,128)S(1)}, f32[64,8,128]{2,1,0:T(8,128)S(1)}, f32[2,64,8,128]{3,2,1,0:T(8,128)S(1)}, f32[2,64,8,128]{3,2,1,0:T(8,128)S(1)...) custom-call(f32[8,1,32,64]{3,2,1,0:T(8,128)} %refs_0_.1, ...), custom_call_target="tpu_custom_call" | custom-call | tf_op jit(solution)/shard_map/exchange/pallas_call | solution.py:430
  9.5 2.5 %relax.1 = f32[8,2,64,128]{3,2,1,0:T(8,128)} custom-call(f32[20,8,128]{2,1,0:T(8,128)S(1)} %get-tuple-element.15.got, f32[64,8,128]{2,1,0:T(8,128)S(1)} %get-tuple-element.16.fine, f32[2,64,8,128]{3,2,1,0:T(8,128)S(1)} %get-tuple-element.17.inner, f32[2,64,8,128]{3,2,1,0:T(8,128)S(1)} %get-tuple-element.18.pin, f32[8,128]{1,0:T(8,128)S(1)} %get-tuple-element.19.rate_ref, ...), custom_call_target="tpu_custom_call" | custom-call | tf_op jit(solution)/shard_map/relax/pallas_call | solution.py:449

commit v9 on v7

--- a/solution.py
+++ b/solution.py
@@ -258,7 +258,7 @@
 
 
 def relax(got, fine, inner, pin, rate_ref, strips_ref, side_pin, main_ref, strip_ref, label_ref, *rest):
-    out_hbm, out_ref, out_sem = rest
+    (out_ref,) = rest
     fy, phases, width = fine.shape
     ny, nz = fy // 2, width // 2
     shape = (phases, width)
@@ -372,22 +372,16 @@
         near = near + 2.0 * rim1[y][1 - n]
         return c + rate * (near - c * (6.0 + total(c))) + pinned(n, y)
 
-    chunks, _, _, tall, _ = out_ref.shape
-    out_rows = out_ref.reshape(chunks * phases * 2 * tall, width)
-    copies = []
-    for chunk in range(chunks):
-        for n in range(2):
-            for j in range(tall):
-                at = (chunk * phases * 2 + n) * tall + j
-                row = second_row(n, chunk * tall + j)
-                out_rows[pl.ds(at, phases, stride=2 * tall)] = row
-        copy = pltpu.make_async_copy(
-            out_ref.at[chunk], out_hbm.at[:, :, pl.ds(chunk * tall, tall)], out_sem.at[chunk]
-        )
-        copy.start()
-        copies.append(copy)
-    for copy in copies:
-        copy.wait()
+    out_rows = out_ref.reshape(phases * 2 * fy, width)
+    for n in range(2):
+        for y in range(fy):
+            out_rows[pl.ds(n * fy + y, phases, stride=2 * fy)] = second_row(n, y)
+
+
+def whole(gy, gz, *refs):
+    sources, out_ref, shared, rest = refs[:6], refs[6], refs[7:17], refs[17:]
+    exchange(gy, gz, *sources, *shared, *rest)
+    relax(*shared, out_ref)
 
 
 def shards(gy, gz, coarse, labels, mobility):
@@ -411,12 +405,13 @@
         pltpu.VMEM((4, 2, phases, width), F32),
         *(pltpu.VMEM(v.shape, v.dtype) for v in weights),
     ]
-    parts = pl.pallas_call(
-        functools.partial(exchange, gy, gz),
-        out_shape=shared,
+    return pl.pallas_call(
+        functools.partial(whole, gy, gz),
+        out_shape=pltpu.VMEM((phases, 2, 2 * ny, width), F32),
         in_specs=[hbm] * len(sources),
-        out_specs=[vmem] * len(shared),
+        out_specs=vmem,
         scratch_shapes=[
+            *shared,
             pltpu.SMEM(mobility.shape, F32),
             pltpu.VMEM(labels.shape, jnp.int32),
             pltpu.VMEM(coarse.shape, F32),
@@ -426,22 +421,10 @@
             pltpu.SemaphoreType.DMA((len(sources),)),
         ],
         compiler_params=pltpu.CompilerParams(
-            collective_id=0, has_side_effects=True, vmem_limit_bytes=12 * 2**20
+            collective_id=0, has_side_effects=True, vmem_limit_bytes=16 * 2**20
         ),
-        name="exchange",
+        name="relax",
     )(*sources)
-    return pl.pallas_call(
-        relax,
-        out_shape=jax.ShapeDtypeStruct((phases, 2, 2 * ny, width), F32),
-        in_specs=[vmem] * len(shared),
-        out_specs=hbm,
-        scratch_shapes=[
-            pltpu.VMEM((2, phases, 2, ny, width), F32),
-            pltpu.SemaphoreType.DMA((2,)),
-        ],
-        compiler_params=pltpu.CompilerParams(vmem_limit_bytes=12 * 2**20),
-        name="relax",
-    )(*parts)
 
 
 def solution(mesh):

time: 11.5 us -> 11.6 us (level)
  Pallas kernels: 11.4 us -> 10.6 us
  local copies, waits for them, and re-layouts: 0 us -> 0.8 us
    unnamed x0 -> x1, local copies, waits for them, and re-layouts: none -> 0.8 us
    pallas_call x2 -> x1, Pallas kernels: 11.4 us -> 10.6 us  [shards(): pl.pallas_call(functools.partial(whole, gy, gz), out_shape=pltpu.VMEM((ph...]
where the time goes in v9:
time: 11.6 us; the launch traced here: 11.4 us
  Pallas kernels  10.6 us (91%)
  local copies, waits for them, and re-layouts  0.8 us (7%)
    pallas_call x1, Pallas kernels, shards(): pl.pallas_call(functools.partial(whole, gy, gz), out_shape=pltpu.VMEM((ph...  10.6 us
    unnamed x1, local copies, waits for them, and re-layouts  0.8 us

profile of v9, /device:TPU:0, one launch (start us, length us, event | category | flops | bytes accessed | tf_op | source)
XLA Modules:
  0.0 11.4 jit_solution(6608045636769295406)
XLA Ops:
  0.0 10.6 %relax.1 = f32[8,2,64,128]{3,2,1,0:T(8,128)S(1)} custom-call(f32[8,1,32,64]{3,2,1,0:T(8,128)} %refs_0_.1, s32[2,64,128]{2,1,0:T(8,128)} %refs_1_.1, f32[8]{0:T(128)} %refs_2_.1, bf16[128,128]{1,0:T(8,128)(2,1)} %constant.6.clone.refs_3_, bf16[512,1024]{1,0:T(8,128)(2,1)} %constant.7.clone.refs_4_, bf16[256,256]{1,0:T(8,128)(2,1)} %constant.8.clone.refs_5_), custom_call_target="tpu_custom_call" | custom-call | tf_op jit(solution)/shard_map/relax/pallas_call | solution.py:408
  10.6 0.8 %copy.8 = f32[8,2,64,128]{3,2,1,0:T(8,128)} copy(f32[8,2,64,128]{3,2,1,0:T(8,128)S(1)} %relax.1) | data formatting | bytes 1048576

commit v10 on v7

--- a/solution.py
+++ b/solution.py
@@ -373,14 +373,12 @@
         return c + rate * (near - c * (6.0 + total(c))) + pinned(n, y)
 
     chunks, _, _, tall, _ = out_ref.shape
-    out_rows = out_ref.reshape(chunks * phases * 2 * tall, width)
     copies = []
     for chunk in range(chunks):
         for n in range(2):
-            for j in range(tall):
-                at = (chunk * phases * 2 + n) * tall + j
-                row = second_row(n, chunk * tall + j)
-                out_rows[pl.ds(at, phases, stride=2 * tall)] = row
+            for j in range(0, tall, 8):
+                rows = jnp.stack([second_row(n, chunk * tall + j + i) for i in range(8)])
+                out_ref[chunk, :, n, j : j + 8] = jnp.swapaxes(rows, 0, 1)
         copy = pltpu.make_async_copy(
             out_ref.at[chunk], out_hbm.at[:, :, pl.ds(chunk * tall, tall)], out_sem.at[chunk]
         )

time: 11.5 us -> 11.4 us (level)
  Pallas kernels: 11.4 us -> 11.2 us
    pallas_call x1, Pallas kernels: 1.86 us -> 1.7 us  [shards(): pl.pallas_call(relax, out_shape=jax.ShapeDtypeStruct((phases, 2, 2 * ny,...]
where the time goes in v10:
time: 11.4 us; the launch traced here: 11.2 us
  Pallas kernels  11.2 us (98%)
    pallas_call x1, Pallas kernels, shards(): pl.pallas_call(functools.partial(exchange, gy, gz), out_shape=shared, in_...  9.52 us
    pallas_call x1, Pallas kernels, shards(): pl.pallas_call(relax, out_shape=jax.ShapeDtypeStruct((phases, 2, 2 * ny,...  1.7 us

profile of v10, /device:TPU:0, one launch (start us, length us, event | category | flops | bytes accessed | tf_op | source)
XLA Modules:
  0.0 11.2 jit_solution(13868925366311602920)
XLA Ops:
  0.0 9.5 %exchange.1 = (f32[20,8,128]{2,1,0:T(8,128)S(1)}, f32[64,8,128]{2,1,0:T(8,128)S(1)}, f32[2,64,8,128]{3,2,1,0:T(8,128)S(1)}, f32[2,64,8,128]{3,2,1,0:T(8,128)S(1)...) custom-call(f32[8,1,32,64]{3,2,1,0:T(8,128)} %refs_0_.1, ...), custom_call_target="tpu_custom_call" | custom-call | tf_op jit(solution)/shard_map/exchange/pallas_call | solution.py:412
  9.5 1.7 %relax.1 = f32[8,2,64,128]{3,2,1,0:T(8,128)} custom-call(f32[20,8,128]{2,1,0:T(8,128)S(1)} %get-tuple-element.15.got, f32[64,8,128]{2,1,0:T(8,128)S(1)} %get-tuple-element.16.fine, f32[2,64,8,128]{3,2,1,0:T(8,128)S(1)} %get-tuple-element.17.inner, f32[2,64,8,128]{3,2,1,0:T(8,128)S(1)} %get-tuple-element.18.pin, f32[8,128]{1,0:T(8,128)S(1)} %get-tuple-element.19.rate_ref, ...), custom_call_target="tpu_custom_call" | custom-call | tf_op jit(solution)/shard_map/relax/pallas_call | solution.py:431
